TPU v7x, 512 devices: a whole 4x8x8 slice. The times are simulated.
512 devices in a mesh: rows: 64 (over z_hi, y, core), feat: 8 (over x, z_lo).
Axes of the slice: x: 4, y: 8, z: 8 (z_hi: 4, z_lo: 2; z = z_hi * 2 + z_lo), core: 2. Of those that a mesh axis runs over, the one named last changes fastest.
Arguments:
- features: bfloat16 [16384, 6144], P('rows', 'feat'), may hold values from -80 to 80
- labels: int32 [16384], P('rows'), may hold values from 0 to 511
- probe_weight: bfloat16 [6144, 512], P('feat'), may hold values from -1 to 1
- sampled: int32 [14336], P('rows'), may hold values from 0 to 255
Outputs:
- newton_step: bfloat16 [6144, 512], P('feat')
- cg_residual: bfloat16 [6144, 512], P('feat')
All inputs are finite; a program needn't handle non-finite values.
Results may differ from a plain program's by a relative error of at most 0.023.
Values may be sent and summed in bfloat16 or wider, within the bound.
A program may use at most 64 MiB of HBM per device.

v0:
```python
import jax
import jax.numpy as jnp
from jax import lax
from jax.sharding import PartitionSpec as P

damping = 0.01


def body(features, labels, probe_weight, sampled):
    row_count = features.shape[0]
    classes = probe_weight.shape[1]
    partial_value = jnp.dot(features, probe_weight, preferred_element_type=jnp.float32)
    logits = lax.psum(partial_value, "feat")
    probs = jax.nn.softmax(logits, axis=-1)
    onehot = (labels[:, None] == lax.broadcasted_iota(jnp.int32, (row_count, classes), 1)).astype(
        jnp.float32
    )
    total_rows = row_count * lax.axis_size("rows")
    err = ((probs - onehot) / total_rows).astype(jnp.bfloat16)
    local_grad = lax.dot_general(
        features, err, (((0,), (0,)), ((), ())), preferred_element_type=jnp.float32
    )
    damped_probe = damping * probe_weight.astype(jnp.float32)
    grad = lax.psum(local_grad, "rows") + damped_probe
    chosen = jnp.take(features, sampled, axis=0)
    chosen_probs = jnp.take(probs, sampled, axis=0)
    proj_part = jnp.dot(chosen, grad.astype(jnp.bfloat16), preferred_element_type=jnp.float32)
    proj = lax.psum(proj_part.astype(jnp.bfloat16), "feat").astype(jnp.float32)
    total_samples = sampled.shape[0] * lax.axis_size("rows")
    inner = jnp.sum(chosen_probs * proj, axis=-1, keepdims=True)
    weighted = ((chosen_probs * proj - chosen_probs * inner) / total_samples).astype(jnp.bfloat16)
    local_image = lax.dot_general(
        chosen, weighted, (((0,), (0,)), ((), ())), preferred_element_type=jnp.float32
    )
    image = lax.psum(local_image, "rows") + damping * grad
    norm_sq, curv = lax.psum((jnp.sum(grad * grad), jnp.sum(grad * image)), "feat")
    alpha = norm_sq / curv
    return ((-alpha * grad).astype(jnp.bfloat16), (-grad + alpha * image).astype(jnp.bfloat16))


def solution(mesh):
    in_specs = (P("rows", "feat"), P("rows"), P("feat", None), P("rows"))
    out_specs = (P("feat", None), P("feat", None))
    return jax.shard_map(body, mesh=mesh, in_specs=in_specs, out_specs=out_specs, check_vma=False)
```

profile of v0, /device:TPU:1, one launch (start us, length us, event | category | flops | bytes accessed | tf_op | source)
XLA Modules:
  0.0 1345.2 jit_solution(4445755519649457193)
XLA Ops:
  7.2 0.0 copy-start
  7.2 0.0 all-reduce.6.cloned.1.call-start
  7.2 0.9 copy-done
  8.2 2.3 fusion.16
  10.5 0.0 all-reduce.6.cloned.1.call-update
  10.5 0.0 all-reduce.8.cloned.1.call-start
  10.5 87.5 %all-reduce.6.cloned.1.call-done = f32[256,512]{1,0:T(8,128)} async-done(((f32[256,512]{1,0:T(8,128)}), f32[256,512]{1,0:T(8,128)}) %all-reduce.6.cloned.1.call-update) | async-done | bytes 524304 | tf_op jit(solution)/shard_map/psum | solution.py:13
  98.0 1.2 reduce_max.9
  99.2 1.3 fusion.2
  100.4 1.2 fusion.1
  101.7 0.0 copy-start.2
  101.7 1.7 convolution_bitcast_fusion
  103.3 0.0 all-reduce.8.cloned.1.call-update
  103.4 0.0 all-reduce.10.cloned.1.call-start
  103.4 0.3 copy.6
  103.7 0.3 copy-done.5
  104.0 1.1 gather_fusion
  105.2 561.3 %all-reduce.8.cloned.1.call-done = f32[768,512]{0,1:T(8,128)} async-done(((f32[768,512]{0,1:T(8,128)}), f32[768,512]{0,1:T(8,128)}) %all-reduce.8.cloned.1.call-update) | async-done | bytes 1572880 | tf_op jit(solution)/shard_map/psum | solution.py:24
  666.4 2.5 convolution_convert_fusion
  669.0 0.0 all-reduce.10.cloned.1.call-update
  669.0 0.0 all-reduce.12.cloned.1.call-start
  669.1 0.9 gather_fusion.1
  670.0 74.6 %all-reduce.10.cloned.1.call-done = bf16[224,512]{1,0:T(8,128)(2,1)} async-done(((bf16[224,512]{1,0:T(8,128)(2,1)}), bf16[224,512]{1,0:T(8,128)(2,1)}) %all-reduce.10.cloned.1.call-update) | async-done | bytes 229392 | tf_op jit(solution)/shard_map/psum | solution.py:28
  744.6 1.1 fusion.3
  745.7 2.8 fusion.6
  748.5 0.0 all-reduce.12.cloned.1.call-update
  748.5 564.0 %all-reduce.12.cloned.1.call-done = f32[768,512]{0,1:T(8,128)} async-done(((f32[768,512]{0,1:T(8,128)}), f32[768,512]{0,1:T(8,128)}) %all-reduce.12.cloned.1.call-update) | async-done | bytes 1572880 | tf_op jit(solution)/shard_map/psum | solution.py:35
  1312.5 2.5 multiply_reduce_fusion
  1315.0 16.1 %all-reduce = (f32[]{:T(128)}, f32[]{:T(128)}) all-reduce(f32[]{:T(128)} %get-tuple-element.5, f32[]{:T(128)} %get-tuple-element.4), channel_id=1, replica_groups=mesh['rows'=64,'feat'=8] {'feat'}, use_global_device_ids=true, to_apply=%region_5.6 | all-reduce | flops 2 | bytes 16 | tf_op jit(solution)/shard_map/psum | solution.py:36
  1332.4 2.8 add_convert_fusion
  1335.3 2.3 copy.9
  1337.5 1.2 copy.8
  (11 shorter events, 0.0 us)
Async XLA Ops:
  7.2 1.0 copy-start
  7.2 90.8 %all-reduce.6.cloned.1.call-start = ((), (), s32[]{:S(2)}) async-start(), calls=%async_computation | async-start | bytes 1048576 | tf_op jit(solution)/shard_map/psum | solution.py:13
  10.5 91.2 %copy-start.4 = (s32[256]{0:T(256)S(1)}, s32[256]{0:T(256)}, u32[]{:S(2)}) copy-start(s32[256]{0:T(256)} %param.5) | copy-start | bytes 3076
  10.5 656.0 %all-reduce.8.cloned.1.call-start = ((), (), s32[]{:S(2)}) async-start(), calls=%async_computation.1 | async-start | bytes 3145728 | tf_op jit(solution)/shard_map/psum | solution.py:24
  101.7 1.7 copy-start.2
  103.3 0.7 copy-start.5
  103.4 641.2 %all-reduce.10.cloned.1.call-start = ((), (), s32[]{:S(2)}) async-start(), calls=%async_computation.2 | async-start | bytes 458752 | tf_op jit(solution)/shard_map/psum | solution.py:28
  105.2 639.4 %copy-start.3 = (pred[224]{0:T(512)(128)(4,1)}, pred[224]{0:T(512)(128)(4,1)S(1)}, u32[]{:S(2)}) copy-start(pred[224]{0:T(512)(128)(4,1)S(1)} %compare_and_fusion) | copy-start | bytes 676
  669.0 643.5 %all-reduce.12.cloned.1.call-start = ((), (), s32[]{:S(2)}) async-start(), calls=%async_computation.3 | async-start | bytes 3145728 | tf_op jit(solution)/shard_map/psum | solution.py:35
  745.7 566.8 %copy-start.1 = (f32[768,512]{0,1:T(8,128)S(1)}, f32[768,512]{0,1:T(8,128)}, u32[]{:S(2)}) copy-start(f32[768,512]{0,1:T(8,128)} %all-reduce.8.cloned.1.call-done) | copy-start | bytes 4718596
Sparse Core Ops, SparseCore 0:
  11.5 86.4 all-reduce.5
  103.5 562.9 all-reduce.7
  669.9 74.5 all-reduce.9
  748.6 563.7 all-reduce.11
where the time goes:
time: 1350 us
  waiting for transfers between devices  1290 us (96%)
  blocking collectives  16.1 us (1%)
  between operations  15.2 us (1%)
    psum x1, waiting for transfers between devices, body(): image = lax.psum(local_image, 'rows') + damping * grad  564 us
    psum x1, waiting for transfers between devices, body(): grad = lax.psum(local_grad, 'rows') + damped_probe  561 us
    psum x1, waiting for transfers between devices, body(): logits = lax.psum(partial_value, 'feat')  87.5 us
    psum x1, waiting for transfers between devices, body(): proj = lax.psum(proj_part.astype(jnp.bfloat16), 'feat').astype(jnp.float32)  74.6 us
  transfers between devices with their start and end apart: 4, of which 4 were waited for; matrix products, arithmetic and copies ran while one was open for 0% of the time, Pallas kernels for 0%

commit v1 on v0

v1 whole, which is shorter than its diff:
```python
import functools

import jax
import jax.numpy as jnp
from jax import lax
from jax.experimental import pallas as pl
from jax.experimental.pallas import tpu as pltpu
from jax.sharding import PartitionSpec as P

MESH = pl.DeviceIdType.MESH
DAMPING = 0.01
F32, BF16 = jnp.float32, jnp.bfloat16
NF, NZ, NY = 8, 4, 8


def kernel(x_ref, lab_ref, w_ref, smp_ref, step_ref, res_ref, xt, part, got_l, err, probs, g_keep, g_out, g_in, g_sum,
           g_ya, g_zb, g_a2, g_b2, g_za, g_yb, grad_a, grad_b, grad, proj, got_p, wgt, i_keep, i_out, i_in, i_sum,
           i_ya, i_zb, i_a2, i_b2, i_za, i_yb, resid, sc_f, sc_c, sc_y, sc_z, sends, recvs):
    rows = lax.axis_index("rows")
    feat = lax.axis_index("feat")
    core = lax.rem(rows, 2)
    y = lax.rem(rows // 2, NY)
    z = rows // (2 * NY)
    height = x_ref.shape[0]
    own = height // NF
    half = w_ref.shape[1] // 2
    total_rows = height * NF * 8
    total_samples = smp_ref.shape[1] * NF * 8

    def to_feat(k):
        return {"rows": rows, "feat": lax.rem(feat + k, NF)}

    def to_y(k):
        return {"rows": (z * NY + lax.rem(y + k, NY)) * 2 + core, "feat": feat}

    def to_z(k):
        return {"rows": (lax.rem(z + k, NZ) * NY + y) * 2 + core, "feat": feat}

    partner = {"rows": rows + 1 - 2 * core, "feat": feat}
    order_8 = (4, 3, 5, 2, 6, 1, 7)
    order_4 = (2, 1, 3)

    pending = []

    def send(src, dst, where):
        index = len(pending)
        copy = pltpu.make_async_remote_copy(
            src_ref=src, dst_ref=dst, send_sem=sends.at[index], recv_sem=recvs.at[index], device_id=where,
            device_id_type=MESH,
        )
        copy.start()
        pending.append(copy)
        return copy

    def arrive(copies):
        for copy in copies:
            copy.wait_recv()

    barrier = pltpu.get_barrier_semaphore()
    peers = [partner] + [to_feat(k) for k in order_8] + [to_y(k) for k in order_8] + [to_z(k) for k in order_4]
    for where in peers:
        pl.semaphore_signal(barrier, inc=1, device_id=where, device_id_type=MESH)

    part[...] = jnp.dot(x_ref[...], w_ref[...], preferred_element_type=F32).reshape(part.shape)
    pl.semaphore_wait(barrier, len(peers))
    copies = [send(part.at[lax.rem(feat + k, NF)], got_l.at[feat], to_feat(k)) for k in order_8]
    xt[...] = x_ref[...].T
    row_id = feat * own + lax.broadcasted_iota(jnp.int32, (own, height), 0)
    here = row_id == lax.broadcasted_iota(jnp.int32, (own, height), 1)
    label = jnp.sum(jnp.where(here, lab_ref[...], 0), axis=1, keepdims=True)
    sample_id = feat * own + lax.broadcasted_iota(jnp.int32, (own, smp_ref.shape[1]), 0)
    count = jnp.sum(jnp.where(sample_id == smp_ref[...], 1.0, 0.0), axis=1, keepdims=True)
    got_l[feat] = part[feat]
    arrive(copies)
    logits = got_l[0]
    for k in range(1, NF):
        logits = logits + got_l[k]
    expo = jnp.exp(logits - jnp.max(logits, axis=1, keepdims=True))
    p = expo / jnp.sum(expo, axis=1, keepdims=True)
    probs[...] = p
    onehot = jnp.where(label == lax.broadcasted_iota(jnp.int32, p.shape, 1), 1.0, 0.0)
    e = ((p - onehot) / total_rows).astype(BF16)
    err[0, feat] = e[:, :half]
    err[1, feat] = e[:, half:]
    arrive([send(err.at[:, feat], err.at[:, feat], to_feat(k)) for k in order_8])

    def reduce_rows(mat, keep, out, into, total, ya, zb, a2, b2, za, yb, ride):
        depth = total.shape[0]
        cut = depth * 2 // 3
        out[...] = jnp.dot(xt[...], mat[1 - core].reshape(height, half), preferred_element_type=F32).astype(BF16)
        copies = [send(out, into, partner)]
        extra = ride(0, copies)
        keep[...] = jnp.dot(xt[...], mat[core].reshape(height, half), preferred_element_type=F32)
        arrive(copies)
        total[...] = (keep[...] + into[...].astype(F32)).astype(BF16)
        copies = []
        for k in order_8:
            there = pl.multiple_of(lax.rem(y + k, NY) * 64, 64)
            copies.append(send(total.at[pl.ds(there, 64)], ya.at[y], to_y(k)))
            if k in order_4:
                there = pl.multiple_of(cut + lax.rem(z + k, NZ) * 64, 64)
                copies.append(send(total.at[pl.ds(there, 64)], zb.at[z], to_z(k)))
        ride(1, copies)
        ya[y] = total[pl.ds(pl.multiple_of(y * 64, 64), 64)]
        zb[z] = total[pl.ds(pl.multiple_of(cut + z * 64, 64), 64)]
        arrive(copies)
        a = ya[0].astype(F32)
        for k in range(1, NY):
            a = a + ya[k].astype(F32)
        a = a.astype(BF16)
        for k in range(NZ):
            a2[k] = a[k * 16:(k + 1) * 16]
        b = zb[0].astype(F32)
        for k in range(1, NZ):
            b = b + zb[k].astype(F32)
        b = b.astype(BF16)
        for k in range(NY):
            b2[k] = b[(k // 2) * 16:(k // 2 + 1) * 16, (k % 2) * 128:(k % 2 + 1) * 128]
        copies = []
        for k in order_8:
            copies.append(send(b2.at[lax.rem(y + k, NY)], yb.at[y], to_y(k)))
            if k in order_4:
                copies.append(send(a2.at[lax.rem(z + k, NZ)], za.at[z], to_z(k)))
        ride(2, copies)
        za[z] = a2[z]
        yb[y] = b2[y]
        arrive(copies)
        a = za[0].astype(F32)
        for k in range(1, NZ):
            a = a + za[k].astype(F32)
        b = yb[0].astype(F32)
        for k in range(1, NY):
            b = b + yb[k].astype(F32)
        return a, b

    a_row = pl.multiple_of(y * 64 + z * 16, 16)
    b_row = pl.multiple_of(512 + z * 64 + (y // 2) * 16, 16)
    b_lane = pl.multiple_of(lax.rem(y, 2) * 128, 128)

    def gather_rows(full, a, b):
        at_a = full.at[core, pl.ds(a_row, 16)]
        at_b = full.at[core, pl.ds(b_row, 16), pl.ds(b_lane, 128)]
        at_a[...] = a
        at_b[...] = b
        copies = []
        for k in order_8:
            copies.append(send(at_b, at_b, to_y(k)))
            if k in order_4:
                copies.append(send(at_a, at_a, to_z(k)))
        arrive(copies)
        at_a = full.at[core, pl.ds(pl.multiple_of(y * 64, 64), 64)]
        at_b = full.at[core, pl.ds(pl.multiple_of(512 + z * 64, 64), 64)]
        copies = []
        for k in order_8:
            copies.append(send(at_a, at_a, to_y(k)))
            if k in order_4:
                copies.append(send(at_b, at_b, to_z(k)))
        arrive(copies)
        return [send(full.at[core], full.at[core], partner)]

    a, b = reduce_rows(err, g_keep, g_out, g_in, g_sum, g_ya, g_zb, g_a2, g_b2, g_za, g_yb, lambda *_: None)
    lane = pl.multiple_of(core * half, half)
    a = a + DAMPING * w_ref[pl.ds(a_row, 16), pl.ds(lane, half)].astype(F32)
    b = b + DAMPING * w_ref[pl.ds(b_row, 16), pl.ds(pl.multiple_of(core * half + b_lane, 128), 128)].astype(F32)
    grad_a[...] = a
    grad_b[...] = b
    copies = gather_rows(grad, a.astype(BF16), b.astype(BF16))
    norm = jnp.sum(jnp.sum(a * a, axis=1, keepdims=True), axis=0, keepdims=True) + jnp.sum(
        jnp.sum(b * b, axis=1, keepdims=True), axis=0, keepdims=True)

    def project(side):
        value = jnp.dot(x_ref[...], grad[side], preferred_element_type=F32).astype(BF16)
        proj[side] = value.reshape(proj.shape[1:])
        return [send(proj.at[side, lax.rem(feat + k, NF)], got_p.at[side, feat], to_feat(k)) for k in order_8]

    first = project(core)
    arrive(copies)
    second = project(1 - core)
    got_p[0, feat] = proj[0, feat]
    got_p[1, feat] = proj[1, feat]
    arrive(first + second)
    pj = []
    for side in range(2):
        value = got_p[side, 0].astype(F32)
        for k in range(1, NF):
            value = value + got_p[side, k].astype(F32)
        pj.append(value)
    p0, p1 = probs[:, :half], probs[:, half:]
    pp0, pp1 = p0 * pj[0], p1 * pj[1]
    inner = jnp.sum(pp0, axis=1, keepdims=True) + jnp.sum(pp1, axis=1, keepdims=True)
    scale = count / total_samples
    w0 = ((pp0 - p0 * inner) * scale).astype(BF16)
    w1 = ((pp1 - p1 * inner) * scale).astype(BF16)
    wgt[0, feat] = w0
    wgt[1, feat] = w1
    copies = [send(wgt.at[:, feat], wgt.at[:, feat], to_feat(k)) for k in order_8]
    curv = jnp.sum(jnp.sum(w0.astype(F32) * pj[0] + w1.astype(F32) * pj[1], axis=1, keepdims=True), axis=0, keepdims=True)
    top = lax.broadcasted_iota(jnp.int32, (8, 128), 0) < 4
    sc_f[feat] = jnp.where(top, norm, curv)
    copies += [send(sc_f.at[feat], sc_f.at[feat], to_feat(k)) for k in order_8]
    arrive(copies)

    def ride(stage, copies):
        if stage == 0:
            sc_c[core] = functools.reduce(jnp.add, [sc_f[k] for k in range(NF)])
            copies += [send(sc_c.at[core], sc_c.at[core], partner)]
        if stage == 1:
            sc_y[y] = sc_c[0] + sc_c[1]
            copies += [send(sc_y.at[y], sc_y.at[y], to_y(k)) for k in order_8]
        if stage == 2:
            sc_z[z] = functools.reduce(jnp.add, [sc_y[k] for k in range(NY)])
            copies += [send(sc_z.at[z], sc_z.at[z], to_z(k)) for k in order_4]

    a, b = reduce_rows(wgt, i_keep, i_out, i_in, i_sum, i_ya, i_zb, i_a2, i_b2, i_za, i_yb, ride)
    sums = functools.reduce(jnp.add, [sc_z[k] for k in range(NZ)])
    norm, curv = sums[0:1, 0:1], sums[4:5, 0:1]
    alpha = norm / (curv + DAMPING * norm)
    a = -grad_a[...] + alpha * (a + DAMPING * grad_a[...])
    b = -grad_b[...] + alpha * (b + DAMPING * grad_b[...])
    copies = gather_rows(resid, a.astype(BF16), b.astype(BF16))
    step_ref[:, :half] = (-alpha * grad[0].astype(F32)).astype(BF16)
    step_ref[:, half:] = (-alpha * grad[1].astype(F32)).astype(BF16)
    arrive(copies)
    res_ref[:, :half] = resid[0]
    res_ref[:, half:] = resid[1]
    for copy in pending:
        copy.wait_send()


def body(features, labels, probe_weight, sampled):
    height, depth = features.shape
    classes = probe_weight.shape[1]
    half = classes // 2
    own = height // NF
    vmem = pl.BlockSpec(memory_space=pltpu.VMEM)
    out = jax.ShapeDtypeStruct((depth, classes), BF16)

    def chain():
        return [
            pltpu.VMEM((depth, half), F32),
            pltpu.VMEM((depth, half), BF16),
            pltpu.VMEM((depth, half), BF16),
            pltpu.VMEM((depth, half), BF16),
            pltpu.VMEM((NY, 64, half), BF16),
            pltpu.VMEM((NZ, 64, half), BF16),
            pltpu.VMEM((NZ, 16, half), BF16),
            pltpu.VMEM((NY, 16, 128), BF16),
            pltpu.VMEM((NZ, 16, half), BF16),
            pltpu.VMEM((NY, 16, 128), BF16),
        ]

    return pl.pallas_call(
        kernel,
        out_shape=(out, out),
        in_specs=[vmem] * 4,
        out_specs=(vmem, vmem),
        scratch_shapes=[
            pltpu.VMEM((depth, height), BF16),
            pltpu.VMEM((NF, own, classes), F32),
            pltpu.VMEM((NF, own, classes), F32),
            pltpu.VMEM((2, NF, own, half), BF16),
            pltpu.VMEM((own, classes), F32),
            *chain(),
            pltpu.VMEM((16, half), F32),
            pltpu.VMEM((16, 128), F32),
            pltpu.VMEM((2, depth, half), BF16),
            pltpu.VMEM((2, NF, own, half), BF16),
            pltpu.VMEM((2, NF, own, half), BF16),
            pltpu.VMEM((2, NF, own, half), BF16),
            *chain(),
            pltpu.VMEM((2, depth, half), BF16),
            pltpu.VMEM((NF, 8, 128), F32),
            pltpu.VMEM((2, 8, 128), F32),
            pltpu.VMEM((NY, 8, 128), F32),
            pltpu.VMEM((NZ, 8, 128), F32),
            pltpu.SemaphoreType.DMA((160,)),
            pltpu.SemaphoreType.DMA((160,)),
        ],
        compiler_params=pltpu.CompilerParams(
            collective_id=0, has_side_effects=True, vmem_limit_bytes=40 * 1024 * 1024
        ),
    )(features, labels.reshape(1, height), probe_weight, sampled.reshape(1, sampled.shape[0]))


def solution(mesh):
    in_specs = (P("rows", "feat"), P("rows"), P("feat", None), P("rows"))
    out_specs = (P("feat", None), P("feat", None))
    return jax.shard_map(body, mesh=mesh, in_specs=in_specs, out_specs=out_specs, check_vma=False)
```

time: 1350 us -> 103 us (0.08)
  waiting for transfers between devices: 1290 us -> 0 us
  Pallas kernels: 0 us -> 97.7 us
  blocking collectives: 16.1 us -> 0 us
  between operations: 15.2 us -> 0.66 us
    psum x4 -> x0, waiting for transfers between devices: 1290 us -> none  [the longest x1 564 us: body(): image = lax.psum(local_image, 'rows') + damping * grad]
    pallas_call x0 -> x1, Pallas kernels: none -> 97.7 us  [body(): pl.pallas_call(kernel, out_shape=(out, out), in_specs=[vmem] * 4, out_spe...]
    psum x1 -> x0, blocking collectives: 16.1 us -> none  [body(): lax.psum((jnp.sum(grad * grad), jnp.sum(grad * image)), 'feat')]
  transfers between devices with their start and end apart: 4 -> 0, of which waited for: 4 -> 0; matrix products, arithmetic and copies ran while one was open for 0% -> 0% of each run, Pallas kernels for 0% -> 0%
where the time goes in v1:
time: 103 us
  Pallas kernels  97.7 us (95%)
  local copies, waits for them, and re-layouts  4.57 us (4%)
    pallas_call x1, Pallas kernels, body(): pl.pallas_call(kernel, out_shape=(out, out), in_specs=[vmem] * 4, out_spe...  97.7 us
    unnamed x10, local copies, waits for them, and re-layouts  4.57 us

profile of v1, /device:TPU:1, one launch (start us, length us, event | category | flops | bytes accessed | tf_op | source)
XLA Modules:
  0.0 102.9 jit_solution(12711161426218215621)
XLA Ops:
  0.6 0.0 copy-start.3
  0.6 0.0 copy-start.2
  0.7 0.7 copy-done.3
  1.3 0.0 copy-done.2
  1.3 0.0 copy-start
  1.3 1.1 %copy-done = bf16[768,512]{1,0:T(8,128)(2,1)S(1)} copy-done((bf16[768,512]{1,0:T(8,128)(2,1)S(1)}, bf16[768,512]{1,0:T(8,128)(2,1)}, u32[]{:S(2)}) %copy-start) | copy-done | bytes 786456
  2.5 0.0 copy-start.1
  2.5 1.0 copy-done.1
  3.5 97.7 %shard_map.59 = (bf16[768,512]{1,0:T(8,128)(2,1)S(1)}, bf16[768,512]{1,0:T(8,128)(2,1)S(1)}) custom-call(bf16[256,768]{1,0:T(8,128)(2,1)S(1)} %copy-done.1, s32[1,256]{1,0:T(1,128)S(1)} %bitcast.2, bf16[768,512]{1,0:T(8,128)(2,1)S(1)} %copy-done, s32[1,224]{1,0:T(1,128)S(1)} %bitcast.3), custom_call_target="tpu_custom_call" | custom-call | tf_op jit(solution)/shard_map/pallas_call | solution.py:252
  101.1 0.9 copy.8
  102.0 0.9 copy.9
Async XLA Ops:
  0.6 0.7 copy-start.3
  0.6 0.7 copy-start.2
  1.3 1.1 %copy-start = (bf16[768,512]{1,0:T(8,128)(2,1)S(1)}, bf16[768,512]{1,0:T(8,128)(2,1)}, u32[]{:S(2)}) copy-start(bf16[768,512]{1,0:T(8,128)(2,1)} %w_ref.1) | copy-start | bytes 2359300
  2.5 1.0 copy-start.1

commit v2 on v0

v2 whole, which is shorter than its diff:
```python
import functools

import jax
import jax.numpy as jnp
from jax import lax
from jax.experimental import pallas as pl
from jax.experimental.pallas import tpu as pltpu
from jax.sharding import PartitionSpec as P

MESH = pl.DeviceIdType.MESH
DAMPING = 0.01
F32, BF16 = jnp.float32, jnp.bfloat16
NF, NZ, NY, LANES = 8, 4, 8, 128
VMEM_BYTES = 56 * 1024 * 1024
ORDER_8, ORDER_4 = (4, 3, 5, 2, 6, 1, 7), (2, 1, 3)


def add_all(values):
    return functools.reduce(jnp.add, values)


def total_of(value):
    return jnp.sum(jnp.sum(value, axis=1, keepdims=True), axis=0, keepdims=True)


def kernel(x_hbm, lab_hbm, w_hbm, smp_hbm, step_out, resid_out, step_ref, resid, x_ref, lab_ref, w_ref, smp_ref, xt, part, got_l, err, probs,
           g_keep, g_out, g_in, g_sum, g_y, g_z, grad_own, grad, proj, got_p, wgt, i_keep, i_out, i_in, i_sum, i_y, i_z,
           sc_f, sc_c, sc_y, sc_z, loads, stores, sends, recvs):
    rows = lax.axis_index("rows")
    feat = lax.axis_index("feat")
    core = lax.rem(rows, 2)
    y = lax.rem(rows // 2, NY)
    z = rows // (2 * NY)
    height, depth = x_ref.shape
    own = height // NF
    half = w_ref.shape[1] // 2
    piece = depth // NY
    total_rows = height * NF * 8
    total_samples = smp_ref.shape[1] * NF * 8

    loaded = [pltpu.make_async_copy(src, dst, loads.at[i]) for i, (src, dst) in enumerate(
        ((x_hbm, x_ref), (w_hbm, w_ref), (lab_hbm, lab_ref), (smp_hbm, smp_ref)))]
    for copy in loaded:
        copy.start()

    def to_feat(k):
        return {"rows": rows, "feat": lax.rem(feat + k, NF)}

    def to_y(k):
        return {"rows": (z * NY + lax.rem(y + k, NY)) * 2 + core, "feat": feat}

    def to_z(k):
        return {"rows": (lax.rem(z + k, NZ) * NY + y) * 2 + core, "feat": feat}

    partner = {"rows": rows + 1 - 2 * core, "feat": feat}
    pending = []

    def send(src, dst, where):
        index = len(pending)
        copy = pltpu.make_async_remote_copy(
            src_ref=src, dst_ref=dst, send_sem=sends.at[index], recv_sem=recvs.at[index], device_id=where,
            device_id_type=MESH,
        )
        copy.start()
        pending.append(copy)
        return copy

    def arrive(copies):
        for copy in copies:
            copy.wait_recv()

    barrier = pltpu.get_barrier_semaphore()
    peers = [partner] + [to_feat(k) for k in ORDER_8] + [to_y(k) for k in ORDER_8] + [to_z(k) for k in ORDER_4]
    for where in peers:
        pl.semaphore_signal(barrier, inc=1, device_id=where, device_id_type=MESH)

    loaded[0].wait()
    loaded[1].wait()
    copies = []
    for side in range(2):
        part[side] = jnp.dot(
            x_ref[...], w_ref[:, side * half:(side + 1) * half], preferred_element_type=F32).reshape(part.shape[1:])
        if side == 0:
            pl.semaphore_wait(barrier, len(peers))
        copies += [send(part.at[side, lax.rem(feat + k, NF)], got_l.at[side, feat], to_feat(k)) for k in ORDER_8]
    xt[...] = x_ref[...].T
    loaded[2].wait()
    loaded[3].wait()
    row_id = feat * own + lax.broadcasted_iota(jnp.int32, (own, height), 0)
    here = row_id == lax.broadcasted_iota(jnp.int32, (own, height), 1)
    label = jnp.sum(jnp.where(here, lab_ref[...], 0), axis=1, keepdims=True)
    sample_id = feat * own + lax.broadcasted_iota(jnp.int32, (own, smp_ref.shape[1]), 0)
    count = jnp.sum(jnp.where(sample_id == smp_ref[...], 1.0, 0.0), axis=1, keepdims=True)
    for side in range(2):
        got_l[side, feat] = part[side, feat]
    arrive(copies)
    logits = [add_all([got_l[side, k] for k in range(NF)]) for side in range(2)]
    highest = jnp.max(jnp.maximum(*logits), axis=1, keepdims=True)
    expo = [jnp.exp(value - highest) for value in logits]
    bottom = jnp.sum(expo[0] + expo[1], axis=1, keepdims=True)
    for side in range(2):
        p = expo[side] / bottom
        probs[side] = p
        class_id = side * half + lax.broadcasted_iota(jnp.int32, p.shape, 1)
        err[side, feat] = ((p - jnp.where(label == class_id, 1.0, 0.0)) / total_rows).astype(BF16)
    arrive([send(err.at[:, feat], err.at[:, feat], to_feat(k)) for k in ORDER_8])

    def reduce_rows(mat, keep, out, into, total, by_y, by_z, ride):
        value = jnp.dot(xt[...], mat[1 - core].reshape(height, half), preferred_element_type=F32).astype(BF16)
        copies = []
        for j in range(2):
            out[j] = value[:, j * LANES:(j + 1) * LANES]
            copies.append([send(out.at[j], into.at[j], partner)])
        extra = ride(0, None)
        keep[...] = jnp.dot(xt[...], mat[core].reshape(height, half), preferred_element_type=F32)
        along_y = []
        for j in range(2):
            arrive(copies[j])
            total[j] = (keep[:, j * LANES:(j + 1) * LANES] + into[j].astype(F32)).astype(BF16)
            moves = []
            for k in ORDER_8:
                there = pl.multiple_of(lax.rem(y + k, NY) * piece, piece)
                moves.append(send(total.at[j, pl.ds(there, piece)], by_y.at[j, y], to_y(k)))
            by_y[j, y] = total[j, pl.ds(pl.multiple_of(y * piece, piece), piece)]
            along_y.append(moves)
        extra = ride(1, extra)
        along_z = []
        for j in range(2):
            arrive(along_y[j])
            by_z[j, z] = add_all([by_y[j, k].astype(F32) for k in range(NY)]).astype(BF16)
            along_z.append([send(by_z.at[j, z], by_z.at[j, z], to_z(k)) for k in ORDER_4])
        extra = ride(2, extra)
        for j in range(2):
            arrive(along_z[j])
            if j == 0:
                ride(3, extra)
            yield add_all([by_z[j, k].astype(F32) for k in range(NZ)])

    my_rows = pl.ds(pl.multiple_of(y * piece, piece), piece)

    def gather_y(full, j, value):
        mine = full.at[core, j, my_rows]
        mine[...] = value
        return [send(mine, mine, to_y(k)) for k in ORDER_8]

    def across(full, j):
        return [send(full.at[core, j], full.at[core, j], partner)]

    norm = jnp.zeros((1, 1), F32)
    gathers = []
    for j, value in enumerate(reduce_rows(err, g_keep, g_out, g_in, g_sum, g_y, g_z, lambda *_: None)):
        lane = pl.multiple_of(core * half + j * LANES, LANES)
        value = value + DAMPING * w_ref[my_rows, pl.ds(lane, LANES)].astype(F32)
        gathers.append(gather_y(grad, j, value.astype(BF16)))
        grad_own[j] = value
        norm = norm + total_of(value * value)

    def project(side, j):
        value = jnp.dot(x_ref[...], grad[side, j], preferred_element_type=F32).astype(BF16)
        proj[side, j] = value.reshape(proj.shape[2:])
        return [send(proj.at[side, j, lax.rem(feat + k, NF)], got_p.at[side, j, feat], to_feat(k)) for k in ORDER_8]

    arrivals = []
    for j in range(2):
        arrive(gathers[j])
        copies = across(grad, j)
        arrivals += project(core, j)
        arrive(copies)
        arrivals += project(1 - core, j)
    for side in range(2):
        for j in range(2):
            got_p[side, j, feat] = proj[side, j, feat]
    arrive(arrivals)
    quarters = [(side, j) for side in range(2) for j in range(2)]
    pj = [add_all([got_p[side, j, k].astype(F32) for k in range(NF)]) for side, j in quarters]
    ps = [probs[side, :, j * LANES:(j + 1) * LANES] for side, j in quarters]
    pp = [a * b for a, b in zip(ps, pj)]
    inner = jnp.sum(add_all(pp), axis=1, keepdims=True)
    scale = count / total_samples
    curv = jnp.zeros((1, 1), F32)
    weighted = [((a - b * inner) * scale).astype(BF16) for a, b in zip(pp, ps)]
    for (side, j), value in zip(quarters, weighted):
        wgt[side, feat, :, j * LANES:(j + 1) * LANES] = value
    copies = [send(wgt.at[:, feat], wgt.at[:, feat], to_feat(k)) for k in ORDER_8]
    curv = total_of(add_all([a.astype(F32) * b for a, b in zip(weighted, pj)]))
    top = lax.broadcasted_iota(jnp.int32, (8, LANES), 0) < 4
    sc_f[feat] = jnp.where(top, norm / NZ, curv)
    scalars = [send(sc_f.at[feat], sc_f.at[feat], to_feat(k)) for k in ORDER_8]
    arrive(copies)

    def ride(stage, copies):
        if stage == 0:
            arrive(scalars)
            sc_c[core] = add_all([sc_f[k] for k in range(NF)])
            return [send(sc_c.at[core], sc_c.at[core], partner)]
        arrive(copies)
        if stage == 1:
            sc_y[y] = sc_c[0] + sc_c[1]
            return [send(sc_y.at[y], sc_y.at[y], to_y(k)) for k in ORDER_8]
        if stage == 2:
            sc_z[z] = add_all([sc_y[k] for k in range(NY)])
            return [send(sc_z.at[z], sc_z.at[z], to_z(k)) for k in ORDER_4]
        return None

    gathers = []
    for j, value in enumerate(reduce_rows(wgt, i_keep, i_out, i_in, i_sum, i_y, i_z, ride)):
        if j == 0:
            sums = add_all([sc_z[k] for k in range(NZ)])
            norm, curv = sums[0:1, 0:1], sums[4:5, 0:1]
            alpha = norm / (curv + DAMPING * norm)
        g = grad_own[j]
        gathers.append(gather_y(resid, j, (-g + alpha * (value + DAMPING * g)).astype(BF16)))
    stored = []

    def store(src, dst, side, j):
        lanes = pl.ds(pl.multiple_of((2 * side + j) * LANES, LANES), LANES)
        copy = pltpu.make_async_copy(src.at[side, j], dst.at[:, lanes], stores.at[len(stored)])
        copy.start()
        stored.append(copy)

    for side, j in quarters:
        step_ref[side, j] = (-alpha * grad[side, j].astype(F32)).astype(BF16)
        store(step_ref, step_out, side, j)
    copies = []
    for j in range(2):
        arrive(gathers[j])
        copies.append(across(resid, j))
        store(resid, resid_out, core, j)
    for j in range(2):
        arrive(copies[j])
        store(resid, resid_out, 1 - core, j)
    for copy in stored:
        copy.wait()
    for copy in pending:
        copy.wait_send()


def write(step_ref, resid_ref, step_out, resid_out, sems):
    copies = []
    depth = step_ref.shape[0]
    for src, dst in ((step_ref, step_out), (resid_ref, resid_out)):
        for part in range(4):
            some = pl.ds(part * (depth // 4), depth // 4)
            copies.append(pltpu.make_async_copy(src.at[some], dst.at[some], sems.at[len(copies)]))
    for copy in copies:
        copy.start()
    for copy in copies:
        copy.wait()


def body(features, labels, probe_weight, sampled):
    height, depth = features.shape
    classes = probe_weight.shape[1]
    half = classes // 2
    own = height // NF
    piece = depth // NY
    hbm = pl.BlockSpec(memory_space=pltpu.HBM)
    out = jax.ShapeDtypeStruct((depth, classes), BF16)
    labels = labels.reshape(1, height)
    sampled = sampled.reshape(1, sampled.shape[0])

    def chain():
        return [
            pltpu.VMEM((depth, half), F32),
            pltpu.VMEM((2, depth, LANES), BF16),
            pltpu.VMEM((2, depth, LANES), BF16),
            pltpu.VMEM((2, depth, LANES), BF16),
            pltpu.VMEM((2, NY, piece, LANES), BF16),
            pltpu.VMEM((2, NZ, piece, LANES), BF16),
        ]

    step, resid = pl.pallas_call(
        kernel,
        out_shape=(out, out),
        in_specs=[hbm] * 4,
        out_specs=(hbm, hbm),
        scratch_shapes=[
            pltpu.VMEM((2, 2, depth, LANES), BF16),
            pltpu.VMEM((2, 2, depth, LANES), BF16),
            pltpu.VMEM(features.shape, BF16),
            pltpu.VMEM(labels.shape, jnp.int32),
            pltpu.VMEM(probe_weight.shape, BF16),
            pltpu.VMEM(sampled.shape, jnp.int32),
            pltpu.VMEM((depth, height), BF16),
            pltpu.VMEM((2, NF, own, half), F32),
            pltpu.VMEM((2, NF, own, half), F32),
            pltpu.VMEM((2, NF, own, half), BF16),
            pltpu.VMEM((2, own, half), F32),
            *chain(),
            pltpu.VMEM((2, piece, LANES), F32),
            pltpu.VMEM((2, 2, depth, LANES), BF16),
            pltpu.VMEM((2, 2, NF, own, LANES), BF16),
            pltpu.VMEM((2, 2, NF, own, LANES), BF16),
            pltpu.VMEM((2, NF, own, half), BF16),
            *chain(),
            pltpu.VMEM((NF, 8, LANES), F32),
            pltpu.VMEM((2, 8, LANES), F32),
            pltpu.VMEM((NY, 8, LANES), F32),
            pltpu.VMEM((NZ, 8, LANES), F32),
            pltpu.SemaphoreType.DMA((4,)),
            pltpu.SemaphoreType.DMA((8,)),
            pltpu.SemaphoreType.DMA((192,)),
            pltpu.SemaphoreType.DMA((192,)),
        ],
        compiler_params=pltpu.CompilerParams(
            collective_id=0, has_side_effects=True, vmem_limit_bytes=VMEM_BYTES
        ),
    )(features, labels, probe_weight, sampled)
    return pl.pallas_call(
        write,
        out_shape=(out, out),
        in_specs=[hbm] * 2,
        out_specs=(hbm, hbm),
        scratch_shapes=[pltpu.SemaphoreType.DMA((8,))],
        compiler_params=pltpu.CompilerParams(vmem_limit_bytes=VMEM_BYTES),
    )(step, resid)


def solution(mesh):
    in_specs = (P("rows", "feat"), P("rows"), P("feat", None), P("rows"))
    out_specs = (P("feat", None), P("feat", None))
    return jax.shard_map(body, mesh=mesh, in_specs=in_specs, out_specs=out_specs, check_vma=False)
```

time: 1350 us -> 147 us (0.11)
  waiting for transfers between devices: 1290 us -> 0 us
  Pallas kernels: 0 us -> 147 us
  blocking collectives: 16.1 us -> 0 us
  between operations: 15.2 us -> 0.64 us
    psum x4 -> x0, waiting for transfers between devices: 1290 us -> none  [the longest x1 564 us: body(): image = lax.psum(local_image, 'rows') + damping * grad]
    pallas_call x0 -> x2, Pallas kernels: none -> 147 us  [the longest x1 97.8 us: body(): pl.pallas_call(kernel, out_shape=(out, out), in_specs=[hbm] * 4, out_spec...]
    psum x1 -> x0, blocking collectives: 16.1 us -> none  [body(): lax.psum((jnp.sum(grad * grad), jnp.sum(grad * image)), 'feat')]
  transfers between devices with their start and end apart: 4 -> 0, of which waited for: 4 -> 0; matrix products, arithmetic and copies ran while one was open for 0% -> 0% of each run, Pallas kernels for 0% -> 0%
where the time goes in v2:
time: 147 us
  Pallas kernels  147 us (100%)
    pallas_call x1, Pallas kernels, body(): pl.pallas_call(kernel, out_shape=(out, out), in_specs=[hbm] * 4, out_spec...  97.8 us
    pallas_call x1, Pallas kernels, body(): pl.pallas_call(write, out_shape=(out, out), in_specs=[hbm] * 2, out_specs...  48.8 us

profile of v2, /device:TPU:1, one launch (start us, length us, event | category | flops | bytes accessed | tf_op | source)
XLA Modules:
  0.0 147.3 jit_solution(7273818956756784829)
XLA Ops:
  0.6 97.8 %shard_map.59 = (bf16[768,512]{1,0:T(8,128)(2,1)}, bf16[768,512]{1,0:T(8,128)(2,1)}) custom-call(bf16[256,768]{1,0:T(8,128)(2,1)} %x_hbm.1, s32[1,256]{1,0:T(1,128)} %bitcast.2, bf16[768,512]{1,0:T(8,128)(2,1)} %w_hbm.1, s32[1,224]{1,0:T(1,128)} %bitcast.3), custom_call_target="tpu_custom_call" | custom-call | tf_op jit(solution)/shard_map/pallas_call | solution.py:272
  98.5 48.8 %shard_map.60 = (bf16[768,512]{1,0:T(8,128)(2,1)}, bf16[768,512]{1,0:T(8,128)(2,1)}) custom-call(bf16[768,512]{1,0:T(8,128)(2,1)} %get-tuple-element.4.step_ref, bf16[768,512]{1,0:T(8,128)(2,1)} %get-tuple-element.5.resid_ref), custom_call_target="tpu_custom_call" | custom-call | tf_op jit(solution)/shard_map/pallas_call | solution.py:309

commit v3 on v2

v3 whole, which is shorter than its diff:
```python
import functools

import jax
import jax.numpy as jnp
from jax import lax
from jax.experimental import pallas as pl
from jax.experimental.pallas import tpu as pltpu
from jax.sharding import PartitionSpec as P

MESH = pl.DeviceIdType.MESH
DAMPING = 0.01
F32, BF16 = jnp.float32, jnp.bfloat16
NF, NZ, NY, LANES = 8, 4, 8, 128
VMEM_BYTES = 56 * 1024 * 1024
ORDER_8, ORDER_4 = (4, 3, 5, 2, 6, 1, 7), (2, 1, 3)


def add_all(values):
    return functools.reduce(jnp.add, values)


def total_of(value):
    return jnp.sum(jnp.sum(value, axis=1, keepdims=True), axis=0, keepdims=True)


def kernel(x_hbm, lab_hbm, w_hbm, smp_hbm, step_out, resid_out, step_ref, resid, x_ref, lab_ref, w_ref, smp_ref, xt, part, got_l, err, probs,
           g_keep, g_out, g_in, g_sum, g_ya, g_za, g_zb, g_b, g_yb, grad_a, grad_b, grad, pacc, proj, got_p,
           wgt, i_keep, i_out, i_in, i_sum, i_ya, i_za, i_zb, i_b, i_yb,
           sc_f, sc_c, sc_y, sc_z, loads, stores, sends, recvs):
    rows = lax.axis_index("rows")
    feat = lax.axis_index("feat")
    core = lax.rem(rows, 2)
    y = lax.rem(rows // 2, NY)
    z = rows // (2 * NY)
    height, depth = x_ref.shape
    own = height // NF
    half = w_ref.shape[1] // 2
    top = depth * 2 // 3
    pa, pb = top // NY, (depth - top) // NZ
    total_rows = height * NF * 8
    total_samples = smp_ref.shape[1] * NF * 8

    loaded = [pltpu.make_async_copy(src, dst, loads.at[i]) for i, (src, dst) in enumerate(
        ((x_hbm, x_ref), (w_hbm, w_ref), (lab_hbm, lab_ref), (smp_hbm, smp_ref)))]
    for copy in loaded:
        copy.start()

    def to_feat(k):
        return {"rows": rows, "feat": lax.rem(feat + k, NF)}

    def to_y(k):
        return {"rows": (z * NY + lax.rem(y + k, NY)) * 2 + core, "feat": feat}

    def to_z(k):
        return {"rows": (lax.rem(z + k, NZ) * NY + y) * 2 + core, "feat": feat}

    partner = {"rows": rows + 1 - 2 * core, "feat": feat}
    pending = []

    def send(src, dst, where):
        index = len(pending)
        copy = pltpu.make_async_remote_copy(
            src_ref=src, dst_ref=dst, send_sem=sends.at[index], recv_sem=recvs.at[index], device_id=where,
            device_id_type=MESH,
        )
        copy.start()
        pending.append(copy)
        return copy

    def arrive(copies):
        for copy in copies:
            copy.wait_recv()

    barrier = pltpu.get_barrier_semaphore()
    peers = [partner] + [to_feat(k) for k in ORDER_8] + [to_y(k) for k in ORDER_8] + [to_z(k) for k in ORDER_4]
    for where in peers:
        pl.semaphore_signal(barrier, inc=1, device_id=where, device_id_type=MESH)

    loaded[0].wait()
    loaded[1].wait()
    copies = []
    for side in range(2):
        part[side] = jnp.dot(
            x_ref[...], w_ref[:, side * half:(side + 1) * half], preferred_element_type=F32).reshape(part.shape[1:])
        if side == 0:
            pl.semaphore_wait(barrier, len(peers))
        copies += [send(part.at[side, lax.rem(feat + k, NF)], got_l.at[side, feat], to_feat(k)) for k in ORDER_8]
    xt[...] = x_ref[...].T
    loaded[2].wait()
    loaded[3].wait()
    row_id = feat * own + lax.broadcasted_iota(jnp.int32, (own, height), 0)
    here = row_id == lax.broadcasted_iota(jnp.int32, (own, height), 1)
    label = jnp.sum(jnp.where(here, lab_ref[...], 0), axis=1, keepdims=True)
    sample_id = feat * own + lax.broadcasted_iota(jnp.int32, (own, smp_ref.shape[1]), 0)
    count = jnp.sum(jnp.where(sample_id == smp_ref[...], 1.0, 0.0), axis=1, keepdims=True)
    for side in range(2):
        got_l[side, feat] = part[side, feat]
    arrive(copies)
    logits = [add_all([got_l[side, k] for k in range(NF)]) for side in range(2)]
    highest = jnp.max(jnp.maximum(*logits), axis=1, keepdims=True)
    expo = [jnp.exp(value - highest) for value in logits]
    bottom = jnp.sum(expo[0] + expo[1], axis=1, keepdims=True)
    for side in range(2):
        p = expo[side] / bottom
        probs[side] = p
        class_id = side * half + lax.broadcasted_iota(jnp.int32, p.shape, 1)
        err[side, feat] = ((p - jnp.where(label == class_id, 1.0, 0.0)) / total_rows).astype(BF16)
    arrive([send(err.at[:, feat], err.at[:, feat], to_feat(k)) for k in ORDER_8])

    def rows_at(start, size):
        return pl.ds(pl.multiple_of(start, size), size)

    a_rows = rows_at(y * pa, pa)
    b_rows = rows_at(top + z * pb, pb)
    b_side, b_part = lax.rem(y, 2), rows_at(top + z * pb + (y // 2) * 16, 16)
    both, upper, lower = pl.ds(0, 2), pl.ds(0, top), pl.ds(top, depth - top)

    def sum_rows(mat, full, finish, keep, out, into, total, ya, za, zb, b2, yb, ride):
        def times(side, start, stop):
            return jnp.dot(xt[start:stop], mat[side].reshape(height, half), preferred_element_type=F32)

        value = times(1 - core, top, depth).astype(BF16)
        for j in range(2):
            out[j, top:] = value[:, j * LANES:(j + 1) * LANES]
        core_b = [send(out.at[both, lower], into.at[both, lower], partner)]
        value = times(1 - core, 0, top).astype(BF16)
        core_a = []
        for j in range(2):
            out[j, :top] = value[:, j * LANES:(j + 1) * LANES]
            core_a.append([send(out.at[j, upper], into.at[j, upper], partner)])
        extra = ride(0, None)
        for start, stop in ((top, depth), (0, top)):
            value = times(core, start, stop)
            for j in range(2):
                keep[j, start:stop] = value[:, j * LANES:(j + 1) * LANES]
        extra = ride(1, extra)

        arrive(core_b)
        for j in range(2):
            total[j, top:] = (keep[j, top:] + into[j, top:].astype(F32)).astype(BF16)
        to_zb = []
        for k in ORDER_4:
            there = rows_at(top + lax.rem(z + k, NZ) * pb, pb)
            to_zb.append(send(total.at[both, there], zb.at[z], to_z(k)))
        to_ya = []
        for j in range(2):
            arrive(core_a[j])
            total[j, :top] = (keep[j, :top] + into[j, :top].astype(F32)).astype(BF16)
            to_ya.append([send(total.at[j, rows_at(lax.rem(y + k, NY) * pa, pa)], ya.at[j, y], to_y(k)) for k in ORDER_8])
        zb[z] = total[both, b_rows]
        for j in range(2):
            ya[j, y] = total[j, a_rows]

        arrive(to_zb)
        b2[...] = add_all([zb[k].astype(F32) for k in range(NZ)]).astype(BF16)
        to_yb = []
        for k in ORDER_8:
            there = lax.rem(y + k, NY)
            to_yb.append(send(b2.at[lax.rem(there, 2), rows_at((there // 2) * 16, 16)], yb.at[y], to_y(k)))
        yb[y] = b2[b_side, rows_at((y // 2) * 16, 16)]
        to_za = []
        for j in range(2):
            arrive(to_ya[j])
            za[j, z] = add_all([ya[j, k].astype(F32) for k in range(NY)]).astype(BF16)
            to_za.append([send(za.at[j, z], za.at[j, z], to_z(k)) for k in ORDER_4])
            if j == 0:
                extra = ride(2, extra)

        arrive(to_yb)
        ride(3, extra)
        mine = full.at[core, b_side, b_part]
        mine[...] = finish(2, add_all([yb[k].astype(F32) for k in range(NY)])).astype(BF16)
        from_yb = [send(mine, mine, to_y(k)) for k in ORDER_8]
        from_ya = []
        for j in range(2):
            arrive(to_za[j])
            mine = full.at[core, j, a_rows]
            mine[...] = finish(j, add_all([za[j, k].astype(F32) for k in range(NZ)])).astype(BF16)
            from_ya.append([send(mine, mine, to_y(k)) for k in ORDER_8])

        arrive(from_yb)
        mine = full.at[core, both, b_rows]
        from_zb = [send(mine, mine, to_z(k)) for k in ORDER_4]
        across = []
        for j in range(2):
            arrive(from_ya[j])
            mine = full.at[core, j, upper]
            across.append([send(mine, mine, partner)])
            yield core, j, across[j]
        for j in range(2):
            arrive(across[j])
        yield 1 - core, 0, None
        arrive(from_zb)
        mine = full.at[core, both, lower]
        across = [send(mine, mine, partner)]
        yield core, 2, None
        arrive(across)
        yield 1 - core, 2, None

    norms = []

    def damped(part, value):
        if part < 2:
            lane = pl.multiple_of(core * half + part * LANES, LANES)
            value = value + DAMPING * w_ref[a_rows, pl.ds(lane, LANES)].astype(F32)
            grad_a[part] = value
            norms.append(total_of(value * value) / NZ)
        else:
            lane = pl.multiple_of(core * half + b_side * LANES, LANES)
            value = value + DAMPING * w_ref[b_part, pl.ds(lane, LANES)].astype(F32)
            grad_b[...] = value
            norms.append(total_of(value * value))
        return value

    arrivals = []
    for side, part, _ in sum_rows(
            err, grad, damped, g_keep, g_out, g_in, g_sum, g_ya, g_za, g_zb, g_b, g_yb, lambda *_: None):
        here = slice(0, top) if part < 2 else slice(top, depth)
        if part == 0 and _ is not None:
            continue
        mat = jnp.concatenate([grad[side, 0, here], grad[side, 1, here]], axis=1)
        value = jnp.dot(x_ref[:, here], mat, preferred_element_type=F32)
        if part < 2:
            pacc[side] = value
        else:
            proj[side] = (pacc[side] + value).astype(BF16).reshape(proj.shape[1:])
            arrivals += [send(proj.at[side, lax.rem(feat + k, NF)], got_p.at[side, feat], to_feat(k)) for k in ORDER_8]
    norm = add_all(norms)
    for side in range(2):
        got_p[side, feat] = proj[side, feat]
    arrive(arrivals)
    quarters = [(side, j) for side in range(2) for j in range(2)]
    pj = [add_all([got_p[side, k, :, j * LANES:(j + 1) * LANES].astype(F32) for k in range(NF)]) for side, j in quarters]
    ps = [probs[side, :, j * LANES:(j + 1) * LANES] for side, j in quarters]
    pp = [a * b for a, b in zip(ps, pj)]
    inner = jnp.sum(add_all(pp), axis=1, keepdims=True)
    scale = count / total_samples
    weighted = [((a - b * inner) * scale).astype(BF16) for a, b in zip(pp, ps)]
    for (side, j), value in zip(quarters, weighted):
        wgt[side, feat, :, j * LANES:(j + 1) * LANES] = value
    copies = [send(wgt.at[:, feat], wgt.at[:, feat], to_feat(k)) for k in ORDER_8]
    curv = total_of(add_all([a.astype(F32) * b for a, b in zip(weighted, pj)]))
    upper_half = lax.broadcasted_iota(jnp.int32, (8, LANES), 0) < 4
    sc_f[feat] = jnp.where(upper_half, norm, curv)
    scalars = [send(sc_f.at[feat], sc_f.at[feat], to_feat(k)) for k in ORDER_8]
    arrive(copies)

    alpha = []

    def ride(stage, copies):
        if stage == 0:
            arrive(scalars)
            sc_c[core] = add_all([sc_f[k] for k in range(NF)])
            return [send(sc_c.at[core], sc_c.at[core], partner)]
        arrive(copies)
        if stage == 1:
            sc_y[y] = sc_c[0] + sc_c[1]
            return [send(sc_y.at[y], sc_y.at[y], to_y(k)) for k in ORDER_8]
        if stage == 2:
            sc_z[z] = add_all([sc_y[k] for k in range(NY)])
            return [send(sc_z.at[z], sc_z.at[z], to_z(k)) for k in ORDER_4]
        sums = add_all([sc_z[k] for k in range(NZ)])
        alpha.append(sums[0:1, 0:1] / (sums[4:5, 0:1] + DAMPING * sums[0:1, 0:1]))
        return None

    def residual(part, value):
        g = grad_a[part] if part < 2 else grad_b[...]
        return -g + alpha[0] * (value + DAMPING * g)

    stored = []

    def store(src, dst, side, j, here):
        lanes = pl.ds(pl.multiple_of((2 * side + j) * LANES, LANES), LANES)
        copy = pltpu.make_async_copy(src.at[side, j, here], dst.at[here, lanes], stores.at[len(stored)])
        copy.start()
        stored.append(copy)

    first = True
    for side, part, _ in sum_rows(
            wgt, resid, residual, i_keep, i_out, i_in, i_sum, i_ya, i_za, i_zb, i_b, i_yb, ride):
        if first:
            first = False
            for one, j in quarters:
                step_ref[one, j] = (-alpha[0] * grad[one, j].astype(F32)).astype(BF16)
                store(step_ref, step_out, one, j, pl.ds(0, depth))
        if part == 2:
            for j in range(2):
                store(resid, resid_out, side, j, lower)
        elif _ is not None:
            store(resid, resid_out, side, part, upper)
        else:
            for j in range(2):
                store(resid, resid_out, side, j, upper)
    for copy in stored:
        copy.wait()
    for copy in pending:
        copy.wait_send()


def write(step_ref, resid_ref, step_out, resid_out, held, ins, outs):
    depth = step_ref.shape[0]
    loads, stores = [], []
    for n, (src, dst) in enumerate(((step_ref, step_out), (resid_ref, resid_out))):
        for part in range(4):
            some = pl.ds(part * (depth // 4), depth // 4)
            index = len(loads)
            loads.append(pltpu.make_async_copy(src.at[some], held.at[n, some], ins.at[index]))
            stores.append(pltpu.make_async_copy(held.at[n, some], dst.at[some], outs.at[index]))
    for copy in loads:
        copy.start()
    for there, back in zip(loads, stores):
        there.wait()
        back.start()
    for copy in stores:
        copy.wait()


def body(features, labels, probe_weight, sampled):
    height, depth = features.shape
    classes = probe_weight.shape[1]
    half = classes // 2
    own = height // NF
    top = depth * 2 // 3
    pa, pb = top // NY, (depth - top) // NZ
    hbm = pl.BlockSpec(memory_space=pltpu.HBM)
    out = jax.ShapeDtypeStruct((depth, classes), BF16)
    labels = labels.reshape(1, height)
    sampled = sampled.reshape(1, sampled.shape[0])

    def chain():
        return [
            pltpu.VMEM((2, depth, LANES), F32),
            pltpu.VMEM((2, depth, LANES), BF16),
            pltpu.VMEM((2, depth, LANES), BF16),
            pltpu.VMEM((2, depth, LANES), BF16),
            pltpu.VMEM((2, NY, pa, LANES), BF16),
            pltpu.VMEM((2, NZ, pa, LANES), BF16),
            pltpu.VMEM((NZ, 2, pb, LANES), BF16),
            pltpu.VMEM((2, pb, LANES), BF16),
            pltpu.VMEM((NY, 16, LANES), BF16),
        ]

    step, resid = pl.pallas_call(
        kernel,
        out_shape=(out, out),
        in_specs=[hbm] * 4,
        out_specs=(hbm, hbm),
        scratch_shapes=[
            pltpu.VMEM((2, 2, depth, LANES), BF16),
            pltpu.VMEM((2, 2, depth, LANES), BF16),
            pltpu.VMEM(features.shape, BF16),
            pltpu.VMEM(labels.shape, jnp.int32),
            pltpu.VMEM(probe_weight.shape, BF16),
            pltpu.VMEM(sampled.shape, jnp.int32),
            pltpu.VMEM((depth, height), BF16),
            pltpu.VMEM((2, NF, own, half), F32),
            pltpu.VMEM((2, NF, own, half), F32),
            pltpu.VMEM((2, NF, own, half), BF16),
            pltpu.VMEM((2, own, half), F32),
            *chain(),
            pltpu.VMEM((2, pa, LANES), F32),
            pltpu.VMEM((16, LANES), F32),
            pltpu.VMEM((2, 2, depth, LANES), BF16),
            pltpu.VMEM((2, height, half), F32),
            pltpu.VMEM((2, NF, own, half), BF16),
            pltpu.VMEM((2, NF, own, half), BF16),
            pltpu.VMEM((2, NF, own, half), BF16),
            *chain(),
            pltpu.VMEM((NF, 8, LANES), F32),
            pltpu.VMEM((2, 8, LANES), F32),
            pltpu.VMEM((NY, 8, LANES), F32),
            pltpu.VMEM((NZ, 8, LANES), F32),
            pltpu.SemaphoreType.DMA((4,)),
            pltpu.SemaphoreType.DMA((16,)),
            pltpu.SemaphoreType.DMA((192,)),
            pltpu.SemaphoreType.DMA((192,)),
        ],
        compiler_params=pltpu.CompilerParams(
            collective_id=0, has_side_effects=True, vmem_limit_bytes=VMEM_BYTES
        ),
    )(features, labels, probe_weight, sampled)
    return pl.pallas_call(
        write,
        out_shape=(out, out),
        in_specs=[hbm] * 2,
        out_specs=(hbm, hbm),
        scratch_shapes=[
            pltpu.VMEM((2, depth, classes), BF16),
            pltpu.SemaphoreType.DMA((8,)),
            pltpu.SemaphoreType.DMA((8,)),
        ],
        compiler_params=pltpu.CompilerParams(vmem_limit_bytes=VMEM_BYTES),
    )(step, resid)


def solution(mesh):
    in_specs = (P("rows", "feat"), P("rows"), P("feat", None), P("rows"))
    out_specs = (P("feat", None), P("feat", None))
    return jax.shard_map(body, mesh=mesh, in_specs=in_specs, out_specs=out_specs, check_vma=False)
```

time: 147 us -> 93.6 us (0.64)
  Pallas kernels: 147 us -> 92.8 us
    pallas_call x1, Pallas kernels: 48.8 us -> 2.29 us  [body(): pl.pallas_call(write, out_shape=(out, out), in_specs=[hbm] * 2, out_specs...]
    pallas_call x1, Pallas kernels: 97.8 us -> 90.5 us  [body(): pl.pallas_call(kernel, out_shape=(out, out), in_specs=[hbm] * 4, out_spec...]
where the time goes in v3:
time: 93.6 us; the launch traced here: 93.5 us
  Pallas kernels  92.8 us (99%)
    pallas_call x1, Pallas kernels, body(): pl.pallas_call(kernel, out_shape=(out, out), in_specs=[hbm] * 4, out_spec...  90.5 us
    pallas_call x1, Pallas kernels, body(): pl.pallas_call(write, out_shape=(out, out), in_specs=[hbm] * 2, out_specs...  2.29 us

profile of v3, /device:TPU:1, one launch (start us, length us, event | category | flops | bytes accessed | tf_op | source)
XLA Modules:
  0.0 93.5 jit_solution(9362709240972547006)
XLA Ops:
  0.6 90.5 %shard_map.59 = (bf16[768,512]{1,0:T(8,128)(2,1)}, bf16[768,512]{1,0:T(8,128)(2,1)}) custom-call(bf16[256,768]{1,0:T(8,128)(2,1)} %x_hbm.1, s32[1,256]{1,0:T(1,128)} %bitcast.2, bf16[768,512]{1,0:T(8,128)(2,1)} %w_hbm.1, s32[1,224]{1,0:T(1,128)} %bitcast.3), custom_call_target="tpu_custom_call" | custom-call | tf_op jit(solution)/shard_map/pallas_call | solution.py:343
  91.2 2.3 %shard_map.60 = (bf16[768,512]{1,0:T(8,128)(2,1)}, bf16[768,512]{1,0:T(8,128)(2,1)}) custom-call(bf16[768,512]{1,0:T(8,128)(2,1)} %get-tuple-element.4.step_ref, bf16[768,512]{1,0:T(8,128)(2,1)} %get-tuple-element.5.resid_ref), custom_call_target="tpu_custom_call" | custom-call | tf_op jit(solution)/shard_map/pallas_call | solution.py:382

commit v4 on v3

--- a/solution.py
+++ b/solution.py
@@ -24,8 +24,8 @@
 
 
 def kernel(x_hbm, lab_hbm, w_hbm, smp_hbm, step_out, resid_out, step_ref, resid, x_ref, lab_ref, w_ref, smp_ref, xt, part, got_l, err, probs,
-           g_keep, g_out, g_in, g_sum, g_ya, g_za, g_zb, g_b, g_yb, grad_a, grad_b, grad, pacc, proj, got_p,
-           wgt, i_keep, i_out, i_in, i_sum, i_ya, i_za, i_zb, i_b, i_yb,
+           g_keep, g_out, g_in, g_sum, g_ya, g_za, g_zb, g_yb, grad_a, grad_b, grad, pacc, proj, got_p,
+           wgt, i_keep, i_out, i_in, i_sum, i_ya, i_za, i_zb, i_yb,
            sc_f, sc_c, sc_y, sc_z, loads, stores, sends, recvs):
     rows = lax.axis_index("rows")
     feat = lax.axis_index("feat")
@@ -112,10 +112,9 @@
 
     a_rows = rows_at(y * pa, pa)
     b_rows = rows_at(top + z * pb, pb)
-    b_side, b_part = lax.rem(y, 2), rows_at(top + z * pb + (y // 2) * 16, 16)
     both, upper, lower = pl.ds(0, 2), pl.ds(0, top), pl.ds(top, depth - top)
 
-    def sum_rows(mat, full, finish, keep, out, into, total, ya, za, zb, b2, yb, ride):
+    def sum_rows(mat, full, finish, keep, out, into, total, ya, za, zb, yb, ride):
         def times(side, start, stop):
             return jnp.dot(xt[start:stop], mat[side].reshape(height, half), preferred_element_type=F32)
 
@@ -152,12 +151,8 @@
             ya[j, y] = total[j, a_rows]
 
         arrive(to_zb)
-        b2[...] = add_all([zb[k].astype(F32) for k in range(NZ)]).astype(BF16)
-        to_yb = []
-        for k in ORDER_8:
-            there = lax.rem(y + k, NY)
-            to_yb.append(send(b2.at[lax.rem(there, 2), rows_at((there // 2) * 16, 16)], yb.at[y], to_y(k)))
-        yb[y] = b2[b_side, rows_at((y // 2) * 16, 16)]
+        yb[y] = add_all([zb[k].astype(F32) for k in range(NZ)]).astype(BF16)
+        to_yb = [send(yb.at[y], yb.at[y], to_y(k)) for k in ORDER_8]
         to_za = []
         for j in range(2):
             arrive(to_ya[j])
@@ -166,21 +161,21 @@
             if j == 0:
                 extra = ride(2, extra)
 
-        arrive(to_yb)
         ride(3, extra)
-        mine = full.at[core, b_side, b_part]
-        mine[...] = finish(2, add_all([yb[k].astype(F32) for k in range(NY)])).astype(BF16)
-        from_yb = [send(mine, mine, to_y(k)) for k in ORDER_8]
         from_ya = []
-        for j in range(2):
+
+        def gather_a(j):
             arrive(to_za[j])
             mine = full.at[core, j, a_rows]
             mine[...] = finish(j, add_all([za[j, k].astype(F32) for k in range(NZ)])).astype(BF16)
             from_ya.append([send(mine, mine, to_y(k)) for k in ORDER_8])
 
-        arrive(from_yb)
+        gather_a(0)
+        arrive(to_yb)
         mine = full.at[core, both, b_rows]
+        mine[...] = finish(2, add_all([yb[k].astype(F32) for k in range(NY)])).astype(BF16)
         from_zb = [send(mine, mine, to_z(k)) for k in ORDER_4]
+        gather_a(1)
         across = []
         for j in range(2):
             arrive(from_ya[j])
@@ -206,15 +201,16 @@
             grad_a[part] = value
             norms.append(total_of(value * value) / NZ)
         else:
-            lane = pl.multiple_of(core * half + b_side * LANES, LANES)
-            value = value + DAMPING * w_ref[b_part, pl.ds(lane, LANES)].astype(F32)
+            lane = pl.multiple_of(core * half, half)
+            weight = w_ref[b_rows, pl.ds(lane, half)].astype(F32)
+            value = value + DAMPING * jnp.stack([weight[:, :LANES], weight[:, LANES:]])
             grad_b[...] = value
-            norms.append(total_of(value * value))
+            norms.append(total_of(value[0] * value[0] + value[1] * value[1]) / NY)
         return value
 
     arrivals = []
     for side, part, _ in sum_rows(
-            err, grad, damped, g_keep, g_out, g_in, g_sum, g_ya, g_za, g_zb, g_b, g_yb, lambda *_: None):
+            err, grad, damped, g_keep, g_out, g_in, g_sum, g_ya, g_za, g_zb, g_yb, lambda *_: None):
         here = slice(0, top) if part < 2 else slice(top, depth)
         if part == 0 and _ is not None:
             continue
@@ -277,7 +273,7 @@
 
     first = True
     for side, part, _ in sum_rows(
-            wgt, resid, residual, i_keep, i_out, i_in, i_sum, i_ya, i_za, i_zb, i_b, i_yb, ride):
+            wgt, resid, residual, i_keep, i_out, i_in, i_sum, i_ya, i_za, i_zb, i_yb, ride):
         if first:
             first = False
             for one, j in quarters:
@@ -336,8 +332,7 @@
             pltpu.VMEM((2, NY, pa, LANES), BF16),
             pltpu.VMEM((2, NZ, pa, LANES), BF16),
             pltpu.VMEM((NZ, 2, pb, LANES), BF16),
-            pltpu.VMEM((2, pb, LANES), BF16),
-            pltpu.VMEM((NY, 16, LANES), BF16),
+            pltpu.VMEM((NY, 2, pb, LANES), BF16),
         ]
 
     step, resid = pl.pallas_call(
@@ -359,7 +354,7 @@
             pltpu.VMEM((2, own, half), F32),
             *chain(),
             pltpu.VMEM((2, pa, LANES), F32),
-            pltpu.VMEM((16, LANES), F32),
+            pltpu.VMEM((2, pb, LANES), F32),
             pltpu.VMEM((2, 2, depth, LANES), BF16),
             pltpu.VMEM((2, height, half), F32),
             pltpu.VMEM((2, NF, own, half), BF16),

time: 93.6 us -> 93.1 us (level)
  no operation moved by 1% of the time
where the time goes in v4:
time: 93.1 us; the launch traced here: 92.9 us
  Pallas kernels  92.3 us (99%)
    pallas_call x1, Pallas kernels, body(): pl.pallas_call(kernel, out_shape=(out, out), in_specs=[hbm] * 4, out_spec...  90 us
    pallas_call x1, Pallas kernels, body(): pl.pallas_call(write, out_shape=(out, out), in_specs=[hbm] * 2, out_specs...  2.29 us

profile of v4, /device:TPU:1, one launch (start us, length us, event | category | flops | bytes accessed | tf_op | source)
XLA Modules:
  0.0 92.9 jit_solution(5577471120247862446)
XLA Ops:
  0.6 90.0 %shard_map.59 = (bf16[768,512]{1,0:T(8,128)(2,1)}, bf16[768,512]{1,0:T(8,128)(2,1)}) custom-call(bf16[256,768]{1,0:T(8,128)(2,1)} %x_hbm.1, s32[1,256]{1,0:T(1,128)} %bitcast.2, bf16[768,512]{1,0:T(8,128)(2,1)} %w_hbm.1, s32[1,224]{1,0:T(1,128)} %bitcast.3), custom_call_target="tpu_custom_call" | custom-call | tf_op jit(solution)/shard_map/pallas_call | solution.py:338
  90.6 2.3 %shard_map.60 = (bf16[768,512]{1,0:T(8,128)(2,1)}, bf16[768,512]{1,0:T(8,128)(2,1)}) custom-call(bf16[768,512]{1,0:T(8,128)(2,1)} %get-tuple-element.4.step_ref, bf16[768,512]{1,0:T(8,128)(2,1)} %get-tuple-element.5.resid_ref), custom_call_target="tpu_custom_call" | custom-call | tf_op jit(solution)/shard_map/pallas_call | solution.py:377

commit v5 on v4

--- a/solution.py
+++ b/solution.py
@@ -118,22 +118,27 @@
         def times(side, start, stop):
             return jnp.dot(xt[start:stop], mat[side].reshape(height, half), preferred_element_type=F32)
 
+        value = times(1 - core, 0, top).astype(BF16)
+        core_a = []
+        for j in range(2):
+            out[j, :top] = value[:, j * LANES:(j + 1) * LANES]
+            core_a.append([send(out.at[j, upper], into.at[j, upper], partner)])
         value = times(1 - core, top, depth).astype(BF16)
         for j in range(2):
             out[j, top:] = value[:, j * LANES:(j + 1) * LANES]
         core_b = [send(out.at[both, lower], into.at[both, lower], partner)]
-        value = times(1 - core, 0, top).astype(BF16)
-        core_a = []
-        for j in range(2):
-            out[j, :top] = value[:, j * LANES:(j + 1) * LANES]
-            core_a.append([send(out.at[j, upper], into.at[j, upper], partner)])
         extra = ride(0, None)
-        for start, stop in ((top, depth), (0, top)):
+        for start, stop in ((0, top), (top, depth)):
             value = times(core, start, stop)
             for j in range(2):
                 keep[j, start:stop] = value[:, j * LANES:(j + 1) * LANES]
         extra = ride(1, extra)
 
+        to_ya = []
+        for j in range(2):
+            arrive(core_a[j])
+            total[j, :top] = (keep[j, :top] + into[j, :top].astype(F32)).astype(BF16)
+            to_ya.append([send(total.at[j, rows_at(lax.rem(y + k, NY) * pa, pa)], ya.at[j, y], to_y(k)) for k in ORDER_8])
         arrive(core_b)
         for j in range(2):
             total[j, top:] = (keep[j, top:] + into[j, top:].astype(F32)).astype(BF16)
@@ -141,11 +146,6 @@
         for k in ORDER_4:
             there = rows_at(top + lax.rem(z + k, NZ) * pb, pb)
             to_zb.append(send(total.at[both, there], zb.at[z], to_z(k)))
-        to_ya = []
-        for j in range(2):
-            arrive(core_a[j])
-            total[j, :top] = (keep[j, :top] + into[j, :top].astype(F32)).astype(BF16)
-            to_ya.append([send(total.at[j, rows_at(lax.rem(y + k, NY) * pa, pa)], ya.at[j, y], to_y(k)) for k in ORDER_8])
         zb[z] = total[both, b_rows]
         for j in range(2):
             ya[j, y] = total[j, a_rows]
@@ -297,8 +297,8 @@
     depth = step_ref.shape[0]
     loads, stores = [], []
     for n, (src, dst) in enumerate(((step_ref, step_out), (resid_ref, resid_out))):
-        for part in range(4):
-            some = pl.ds(part * (depth // 4), depth // 4)
+        for part in range(8):
+            some = pl.ds(part * (depth // 8), depth // 8)
             index = len(loads)
             loads.append(pltpu.make_async_copy(src.at[some], held.at[n, some], ins.at[index]))
             stores.append(pltpu.make_async_copy(held.at[n, some], dst.at[some], outs.at[index]))
@@ -381,8 +381,8 @@
         out_specs=(hbm, hbm),
         scratch_shapes=[
             pltpu.VMEM((2, depth, classes), BF16),
-            pltpu.SemaphoreType.DMA((8,)),
-            pltpu.SemaphoreType.DMA((8,)),
+            pltpu.SemaphoreType.DMA((16,)),
+            pltpu.SemaphoreType.DMA((16,)),
         ],
         compiler_params=pltpu.CompilerParams(vmem_limit_bytes=VMEM_BYTES),
     )(step, resid)

time: 93.1 us -> 92.9 us (level)
  no operation moved by 1% of the time
where the time goes in v5:
time: 92.9 us; the launch traced here: 92.7 us
  Pallas kernels  92.1 us (99%)
    pallas_call x1, Pallas kernels, body(): pl.pallas_call(kernel, out_shape=(out, out), in_specs=[hbm] * 4, out_spec...  89.7 us
    pallas_call x1, Pallas kernels, body(): pl.pallas_call(write, out_shape=(out, out), in_specs=[hbm] * 2, out_specs...  2.4 us

profile of v5, /device:TPU:1, one launch (start us, length us, event | category | flops | bytes accessed | tf_op | source)
XLA Modules:
  0.0 92.7 jit_solution(4766873565342965962)
XLA Ops:
  0.6 89.7 %shard_map.59 = (bf16[768,512]{1,0:T(8,128)(2,1)}, bf16[768,512]{1,0:T(8,128)(2,1)}) custom-call(bf16[256,768]{1,0:T(8,128)(2,1)} %x_hbm.1, s32[1,256]{1,0:T(1,128)} %bitcast.2, bf16[768,512]{1,0:T(8,128)(2,1)} %w_hbm.1, s32[1,224]{1,0:T(1,128)} %bitcast.3), custom_call_target="tpu_custom_call" | custom-call | tf_op jit(solution)/shard_map/pallas_call | solution.py:338
  90.3 2.4 %shard_map.60 = (bf16[768,512]{1,0:T(8,128)(2,1)}, bf16[768,512]{1,0:T(8,128)(2,1)}) custom-call(bf16[768,512]{1,0:T(8,128)(2,1)} %get-tuple-element.4.step_ref, bf16[768,512]{1,0:T(8,128)(2,1)} %get-tuple-element.5.resid_ref), custom_call_target="tpu_custom_call" | custom-call | tf_op jit(solution)/shard_map/pallas_call | solution.py:377

commit v6 on v5

--- a/solution.py
+++ b/solution.py
@@ -11,6 +11,7 @@
 DAMPING = 0.01
 F32, BF16 = jnp.float32, jnp.bfloat16
 NF, NZ, NY, LANES = 8, 4, 8, 128
+FULL = 15.0 - 1.0 / 256.0
 VMEM_BYTES = 56 * 1024 * 1024
 ORDER_8, ORDER_4 = (4, 3, 5, 2, 6, 1, 7), (2, 1, 3)
 
@@ -35,6 +36,7 @@
     height, depth = x_ref.shape
     own = height // NF
     half = w_ref.shape[1] // 2
+    tiles = own // 16 * 4
     top = depth * 2 // 3
     pa, pb = top // NY, (depth - top) // NZ
     total_rows = height * NF * 8
@@ -78,13 +80,18 @@
 
     loaded[0].wait()
     loaded[1].wait()
-    copies = []
-    for side in range(2):
-        part[side] = jnp.dot(
-            x_ref[...], w_ref[:, side * half:(side + 1) * half], preferred_element_type=F32).reshape(part.shape[1:])
-        if side == 0:
-            pl.semaphore_wait(barrier, len(peers))
-        copies += [send(part.at[side, lax.rem(feat + k, NF)], got_l.at[side, feat], to_feat(k)) for k in ORDER_8]
+    value = jnp.dot(x_ref[...], w_ref[...], preferred_element_type=F32)
+    largest = jnp.maximum(jnp.max(jnp.abs(value), axis=1, keepdims=True), 1e-30)
+    power = jnp.ceil(jnp.log2(largest) * 16.0)
+    codes = jnp.round(value * jnp.exp2(FULL - power / 16.0)).astype(jnp.int32).astype(jnp.int16)
+    powers = jnp.broadcast_to(power, (height, LANES)).astype(jnp.int32).astype(jnp.int16)
+    for i in range(NF):
+        for r in range(own // 16):
+            for c in range(4):
+                part[i, 4 * r + c] = codes[i * own + 16 * r:i * own + 16 * (r + 1), c * LANES:(c + 1) * LANES]
+            part[i, tiles + r] = powers[i * own + 16 * r:i * own + 16 * (r + 1)]
+    pl.semaphore_wait(barrier, len(peers))
+    copies = [send(part.at[lax.rem(feat + k, NF)], got_l.at[feat], to_feat(k)) for k in ORDER_8]
     xt[...] = x_ref[...].T
     loaded[2].wait()
     loaded[3].wait()
@@ -93,10 +100,16 @@
     label = jnp.sum(jnp.where(here, lab_ref[...], 0), axis=1, keepdims=True)
     sample_id = feat * own + lax.broadcasted_iota(jnp.int32, (own, smp_ref.shape[1]), 0)
     count = jnp.sum(jnp.where(sample_id == smp_ref[...], 1.0, 0.0), axis=1, keepdims=True)
-    for side in range(2):
-        got_l[side, feat] = part[side, feat]
+    got_l[feat] = part[feat]
     arrive(copies)
-    logits = [add_all([got_l[side, k] for k in range(NF)]) for side in range(2)]
+    pieces = range(own // 16)
+    units = [[jnp.exp2(got_l[k, tiles + r].astype(jnp.int32).astype(F32) / 16.0 - FULL) for r in pieces] for k in range(NF)]
+    blocks = []
+    for c in range(4):
+        blocks.append(jnp.concatenate([
+            add_all([got_l[k, 4 * r + c].astype(jnp.int32).astype(F32) * units[k][r] for k in range(NF)])
+            for r in pieces], axis=0))
+    logits = [jnp.concatenate(blocks[2 * side:2 * side + 2], axis=1) for side in range(2)]
     highest = jnp.max(jnp.maximum(*logits), axis=1, keepdims=True)
     expo = [jnp.exp(value - highest) for value in logits]
     bottom = jnp.sum(expo[0] + expo[1], axis=1, keepdims=True)
@@ -297,8 +310,8 @@
     depth = step_ref.shape[0]
     loads, stores = [], []
     for n, (src, dst) in enumerate(((step_ref, step_out), (resid_ref, resid_out))):
-        for part in range(8):
-            some = pl.ds(part * (depth // 8), depth // 8)
+        for part in range(4):
+            some = pl.ds(part * (depth // 4), depth // 4)
             index = len(loads)
             loads.append(pltpu.make_async_copy(src.at[some], held.at[n, some], ins.at[index]))
             stores.append(pltpu.make_async_copy(held.at[n, some], dst.at[some], outs.at[index]))
@@ -348,8 +361,8 @@
             pltpu.VMEM(probe_weight.shape, BF16),
             pltpu.VMEM(sampled.shape, jnp.int32),
             pltpu.VMEM((depth, height), BF16),
-            pltpu.VMEM((2, NF, own, half), F32),
-            pltpu.VMEM((2, NF, own, half), F32),
+            pltpu.VMEM((NF, own // 16 * 5, 16, LANES), jnp.int16),
+            pltpu.VMEM((NF, own // 16 * 5, 16, LANES), jnp.int16),
             pltpu.VMEM((2, NF, own, half), BF16),
             pltpu.VMEM((2, own, half), F32),
             *chain(),

time: 92.9 us -> 91.4 us (0.984)
  Pallas kernels: 92.1 us -> 90.6 us
    pallas_call x1, Pallas kernels: 89.7 us -> 88.2 us  [body(): pl.pallas_call(kernel, out_shape=(out, out), in_specs=[hbm] * 4, out_spec...]
where the time goes in v6:
time: 91.4 us; the launch traced here: 91.2 us
  Pallas kernels  90.6 us (99%)
    pallas_call x1, Pallas kernels, body(): pl.pallas_call(kernel, out_shape=(out, out), in_specs=[hbm] * 4, out_spec...  88.2 us
    pallas_call x1, Pallas kernels, body(): pl.pallas_call(write, out_shape=(out, out), in_specs=[hbm] * 2, out_specs...  2.44 us

profile of v6, /device:TPU:1, one launch (start us, length us, event | category | flops | bytes accessed | tf_op | source)
XLA Modules:
  0.0 91.2 jit_solution(15818869935754076005)
XLA Ops:
  0.6 88.2 %shard_map.59 = (bf16[768,512]{1,0:T(8,128)(2,1)}, bf16[768,512]{1,0:T(8,128)(2,1)}) custom-call(bf16[256,768]{1,0:T(8,128)(2,1)} %x_hbm.1, s32[1,256]{1,0:T(1,128)} %bitcast.2, bf16[768,512]{1,0:T(8,128)(2,1)} %w_hbm.1, s32[1,224]{1,0:T(1,128)} %bitcast.3), custom_call_target="tpu_custom_call" | custom-call | tf_op jit(solution)/shard_map/pallas_call | solution.py:351
  88.8 2.4 %shard_map.60 = (bf16[768,512]{1,0:T(8,128)(2,1)}, bf16[768,512]{1,0:T(8,128)(2,1)}) custom-call(bf16[768,512]{1,0:T(8,128)(2,1)} %get-tuple-element.4.step_ref, bf16[768,512]{1,0:T(8,128)(2,1)} %get-tuple-element.5.resid_ref), custom_call_target="tpu_custom_call" | custom-call | tf_op jit(solution)/shard_map/pallas_call | solution.py:390

commit v7 on v6

--- a/solution.py
+++ b/solution.py
@@ -24,10 +24,10 @@
     return jnp.sum(jnp.sum(value, axis=1, keepdims=True), axis=0, keepdims=True)
 
 
-def kernel(x_hbm, lab_hbm, w_hbm, smp_hbm, step_out, resid_out, step_ref, resid, x_ref, lab_ref, w_ref, smp_ref, xt, part, got_l, err, probs,
-           g_keep, g_out, g_in, g_sum, g_ya, g_za, g_zb, g_yb, grad_a, grad_b, grad, pacc, proj, got_p,
-           wgt, i_keep, i_out, i_in, i_sum, i_ya, i_za, i_zb, i_yb,
-           sc_f, sc_c, sc_y, sc_z, loads, stores, sends, recvs):
+def kernel(x_hbm, lab_hbm, w_hbm, smp_hbm, step_out, resid_out, step_ref, resid, x_ref, lab_ref, w_ref, smp_ref, x_other, xt, part, got_l, err_out, err, probs,
+           g_sum, g_ya, g_za, g_zb, g_yb, grad_a, grad_b, grad, pacc, proj, got_p,
+           wgt_out, wgt, i_sum, i_ya, i_za, i_zb, i_yb,
+           sc_own, sc_f, sc_y, sc_z, loads, stores, sends, recvs):
     rows = lax.axis_index("rows")
     feat = lax.axis_index("feat")
     core = lax.rem(rows, 2)
@@ -57,6 +57,10 @@
         return {"rows": (lax.rem(z + k, NZ) * NY + y) * 2 + core, "feat": feat}
 
     partner = {"rows": rows + 1 - 2 * core, "feat": feat}
+
+    def to_other(k):
+        return {"rows": rows + 1 - 2 * core, "feat": lax.rem(feat + k, NF)}
+
     pending = []
 
     def send(src, dst, where):
@@ -74,7 +78,8 @@
             copy.wait_recv()
 
     barrier = pltpu.get_barrier_semaphore()
-    peers = [partner] + [to_feat(k) for k in ORDER_8] + [to_y(k) for k in ORDER_8] + [to_z(k) for k in ORDER_4]
+    peers = [to_y(4), to_z(2)] + [to_y(k) for k in (3, 5)] + [to_feat(k) for k in (3, 5, 4)]
+    peers += [to_other(k) for k in ORDER_8] + [to_z(1), to_z(3), to_y(2), to_y(6)] + [to_feat(k) for k in (2, 6, 1, 7)] + [to_y(1), to_y(7), partner]
     for where in peers:
         pl.semaphore_signal(barrier, inc=1, device_id=where, device_id_type=MESH)
 
@@ -92,7 +97,8 @@
             part[i, tiles + r] = powers[i * own + 16 * r:i * own + 16 * (r + 1)]
     pl.semaphore_wait(barrier, len(peers))
     copies = [send(part.at[lax.rem(feat + k, NF)], got_l.at[feat], to_feat(k)) for k in ORDER_8]
-    xt[...] = x_ref[...].T
+    copy_x = send(x_ref, x_other, partner)
+    xt[:, :height] = x_ref[...].T
     loaded[2].wait()
     loaded[3].wait()
     row_id = feat * own + lax.broadcasted_iota(jnp.int32, (own, height), 0)
@@ -101,6 +107,8 @@
     sample_id = feat * own + lax.broadcasted_iota(jnp.int32, (own, smp_ref.shape[1]), 0)
     count = jnp.sum(jnp.where(sample_id == smp_ref[...], 1.0, 0.0), axis=1, keepdims=True)
     got_l[feat] = part[feat]
+    arrive([copy_x])
+    xt[:, height:] = x_other[...].T
     arrive(copies)
     pieces = range(own // 16)
     units = [[jnp.exp2(got_l[k, tiles + r].astype(jnp.int32).astype(F32) / 16.0 - FULL) for r in pieces] for k in range(NF)]
@@ -117,8 +125,17 @@
         p = expo[side] / bottom
         probs[side] = p
         class_id = side * half + lax.broadcasted_iota(jnp.int32, p.shape, 1)
-        err[side, feat] = ((p - jnp.where(label == class_id, 1.0, 0.0)) / total_rows).astype(BF16)
-    arrive([send(err.at[:, feat], err.at[:, feat], to_feat(k)) for k in ORDER_8])
+        err_out[lax.rem(core + side, 2)] = ((p - jnp.where(label == class_id, 1.0, 0.0)) / total_rows).astype(BF16)
+
+    def to_chips(out, into):
+        copies = [send(out.at[1], into.at[1, feat], partner)]
+        for k in ORDER_8:
+            copies.append(send(out.at[0], into.at[0, feat], to_feat(k)))
+            copies.append(send(out.at[1], into.at[1, feat], to_other(k)))
+        into[0, feat] = out[0]
+        return copies
+
+    arrive(to_chips(err_out, err))
 
     def rows_at(start, size):
         return pl.ds(pl.multiple_of(start, size), size)
@@ -127,34 +144,18 @@
     b_rows = rows_at(top + z * pb, pb)
     both, upper, lower = pl.ds(0, 2), pl.ds(0, top), pl.ds(top, depth - top)
 
-    def sum_rows(mat, full, finish, keep, out, into, total, ya, za, zb, yb, ride):
-        def times(side, start, stop):
-            return jnp.dot(xt[start:stop], mat[side].reshape(height, half), preferred_element_type=F32)
-
-        value = times(1 - core, 0, top).astype(BF16)
-        core_a = []
-        for j in range(2):
-            out[j, :top] = value[:, j * LANES:(j + 1) * LANES]
-            core_a.append([send(out.at[j, upper], into.at[j, upper], partner)])
-        value = times(1 - core, top, depth).astype(BF16)
-        for j in range(2):
-            out[j, top:] = value[:, j * LANES:(j + 1) * LANES]
-        core_b = [send(out.at[both, lower], into.at[both, lower], partner)]
-        extra = ride(0, None)
-        for start, stop in ((0, top), (top, depth)):
-            value = times(core, start, stop)
+    def sum_rows(mat, full, finish, total, ya, za, zb, yb, ride):
+        def times(start, stop):
+            value = jnp.dot(xt[start:stop], mat[...].reshape(2 * height, half), preferred_element_type=F32).astype(BF16)
             for j in range(2):
-                keep[j, start:stop] = value[:, j * LANES:(j + 1) * LANES]
-        extra = ride(1, extra)
-
+                total[j, start:stop] = value[:, j * LANES:(j + 1) * LANES]
+
+        times(0, top)
+        extra = ride(1, None)
         to_ya = []
         for j in range(2):
-            arrive(core_a[j])
-            total[j, :top] = (keep[j, :top] + into[j, :top].astype(F32)).astype(BF16)
             to_ya.append([send(total.at[j, rows_at(lax.rem(y + k, NY) * pa, pa)], ya.at[j, y], to_y(k)) for k in ORDER_8])
-        arrive(core_b)
-        for j in range(2):
-            total[j, top:] = (keep[j, top:] + into[j, top:].astype(F32)).astype(BF16)
+        times(top, depth)
         to_zb = []
         for k in ORDER_4:
             there = rows_at(top + lax.rem(z + k, NZ) * pb, pb)
@@ -189,6 +190,7 @@
         mine[...] = finish(2, add_all([yb[k].astype(F32) for k in range(NY)])).astype(BF16)
         from_zb = [send(mine, mine, to_z(k)) for k in ORDER_4]
         gather_a(1)
+        ride(4, None)
         across = []
         for j in range(2):
             arrive(from_ya[j])
@@ -223,7 +225,7 @@
 
     arrivals = []
     for side, part, _ in sum_rows(
-            err, grad, damped, g_keep, g_out, g_in, g_sum, g_ya, g_za, g_zb, g_yb, lambda *_: None):
+            err, grad, damped, g_sum, g_ya, g_za, g_zb, g_yb, lambda *_: None):
         here = slice(0, top) if part < 2 else slice(top, depth)
         if part == 0 and _ is not None:
             continue
@@ -246,30 +248,38 @@
     scale = count / total_samples
     weighted = [((a - b * inner) * scale).astype(BF16) for a, b in zip(pp, ps)]
     for (side, j), value in zip(quarters, weighted):
-        wgt[side, feat, :, j * LANES:(j + 1) * LANES] = value
-    copies = [send(wgt.at[:, feat], wgt.at[:, feat], to_feat(k)) for k in ORDER_8]
+        wgt_out[lax.rem(core + side, 2), :, j * LANES:(j + 1) * LANES] = value
+    copies = to_chips(wgt_out, wgt)
     curv = total_of(add_all([a.astype(F32) * b for a, b in zip(weighted, pj)]))
     upper_half = lax.broadcasted_iota(jnp.int32, (8, LANES), 0) < 4
-    sc_f[feat] = jnp.where(upper_half, norm, curv)
-    scalars = [send(sc_f.at[feat], sc_f.at[feat], to_feat(k)) for k in ORDER_8]
+    sc_own[...] = jnp.where(upper_half, norm, curv)
+    scalars = [send(sc_own, sc_f.at[1, feat], partner)]
+    for k in ORDER_8:
+        scalars.append(send(sc_own, sc_f.at[0, feat], to_feat(k)))
+        scalars.append(send(sc_own, sc_f.at[1, feat], to_other(k)))
+    sc_f[0, feat] = sc_own[...]
     arrive(copies)
 
     alpha = []
 
     def ride(stage, copies):
-        if stage == 0:
+        if stage == 1:
             arrive(scalars)
-            sc_c[core] = add_all([sc_f[k] for k in range(NF)])
-            return [send(sc_c.at[core], sc_c.at[core], partner)]
-        arrive(copies)
-        if stage == 1:
-            sc_y[y] = sc_c[0] + sc_c[1]
+            both_cores = [add_all([sc_f[lax.rem(core + one, 2), k] for k in range(NF)]) for one in range(2)]
+            sc_y[y] = both_cores[0] + both_cores[1]
             return [send(sc_y.at[y], sc_y.at[y], to_y(k)) for k in ORDER_8]
+        if copies:
+            arrive(copies)
         if stage == 2:
             sc_z[z] = add_all([sc_y[k] for k in range(NY)])
             return [send(sc_z.at[z], sc_z.at[z], to_z(k)) for k in ORDER_4]
-        sums = add_all([sc_z[k] for k in range(NZ)])
-        alpha.append(sums[0:1, 0:1] / (sums[4:5, 0:1] + DAMPING * sums[0:1, 0:1]))
+        if stage == 3:
+            sums = add_all([sc_z[k] for k in range(NZ)])
+            alpha.append(sums[0:1, 0:1] / (sums[4:5, 0:1] + DAMPING * sums[0:1, 0:1]))
+        else:
+            for side, j in quarters:
+                step_ref[side, j] = (-alpha[0] * grad[side, j].astype(F32)).astype(BF16)
+                store(step_ref, step_out, side, j, pl.ds(0, depth))
         return None
 
     def residual(part, value):
@@ -284,14 +294,8 @@
         copy.start()
         stored.append(copy)
 
-    first = True
     for side, part, _ in sum_rows(
-            wgt, resid, residual, i_keep, i_out, i_in, i_sum, i_ya, i_za, i_zb, i_yb, ride):
-        if first:
-            first = False
-            for one, j in quarters:
-                step_ref[one, j] = (-alpha[0] * grad[one, j].astype(F32)).astype(BF16)
-                store(step_ref, step_out, one, j, pl.ds(0, depth))
+            wgt, resid, residual, i_sum, i_ya, i_za, i_zb, i_yb, ride):
         if part == 2:
             for j in range(2):
                 store(resid, resid_out, side, j, lower)
@@ -338,9 +342,6 @@
 
     def chain():
         return [
-            pltpu.VMEM((2, depth, LANES), F32),
-            pltpu.VMEM((2, depth, LANES), BF16),
-            pltpu.VMEM((2, depth, LANES), BF16),
             pltpu.VMEM((2, depth, LANES), BF16),
             pltpu.VMEM((2, NY, pa, LANES), BF16),
             pltpu.VMEM((2, NZ, pa, LANES), BF16),
@@ -360,9 +361,11 @@
             pltpu.VMEM(labels.shape, jnp.int32),
             pltpu.VMEM(probe_weight.shape, BF16),
             pltpu.VMEM(sampled.shape, jnp.int32),
-            pltpu.VMEM((depth, height), BF16),
+            pltpu.VMEM(features.shape, BF16),
+            pltpu.VMEM((depth, 2 * height), BF16),
             pltpu.VMEM((NF, own // 16 * 5, 16, LANES), jnp.int16),
             pltpu.VMEM((NF, own // 16 * 5, 16, LANES), jnp.int16),
+            pltpu.VMEM((2, own, half), BF16),
             pltpu.VMEM((2, NF, own, half), BF16),
             pltpu.VMEM((2, own, half), F32),
             *chain(),
@@ -372,16 +375,17 @@
             pltpu.VMEM((2, height, half), F32),
             pltpu.VMEM((2, NF, own, half), BF16),
             pltpu.VMEM((2, NF, own, half), BF16),
+            pltpu.VMEM((2, own, half), BF16),
             pltpu.VMEM((2, NF, own, half), BF16),
             *chain(),
-            pltpu.VMEM((NF, 8, LANES), F32),
-            pltpu.VMEM((2, 8, LANES), F32),
+            pltpu.VMEM((8, LANES), F32),
+            pltpu.VMEM((2, NF, 8, LANES), F32),
             pltpu.VMEM((NY, 8, LANES), F32),
             pltpu.VMEM((NZ, 8, LANES), F32),
             pltpu.SemaphoreType.DMA((4,)),
             pltpu.SemaphoreType.DMA((16,)),
-            pltpu.SemaphoreType.DMA((192,)),
-            pltpu.SemaphoreType.DMA((192,)),
+            pltpu.SemaphoreType.DMA((208,)),
+            pltpu.SemaphoreType.DMA((208,)),
         ],
         compiler_params=pltpu.CompilerParams(
             collective_id=0, has_side_effects=True, vmem_limit_bytes=VMEM_BYTES

time: 91.4 us -> 90.2 us (0.987)
  Pallas kernels: 90.6 us -> 89.4 us
    pallas_call x1, Pallas kernels: 88.2 us -> 87 us  [body(): pl.pallas_call(kernel, out_shape=(out, out), in_specs=[hbm] * 4, out_spec...]
where the time goes in v7:
time: 90.2 us; the launch traced here: 90 us
  Pallas kernels  89.4 us (99%)
    pallas_call x1, Pallas kernels, body(): pl.pallas_call(kernel, out_shape=(out, out), in_specs=[hbm] * 4, out_spec...  87 us
    pallas_call x1, Pallas kernels, body(): pl.pallas_call(write, out_shape=(out, out), in_specs=[hbm] * 2, out_specs...  2.44 us

profile of v7, /device:TPU:1, one launch (start us, length us, event | category | flops | bytes accessed | tf_op | source)
XLA Modules:
  0.0 90.0 jit_solution(17130486336563416121)
XLA Ops:
  0.6 87.0 %shard_map.59 = (bf16[768,512]{1,0:T(8,128)(2,1)}, bf16[768,512]{1,0:T(8,128)(2,1)}) custom-call(bf16[256,768]{1,0:T(8,128)(2,1)} %x_hbm.1, s32[1,256]{1,0:T(1,128)} %bitcast.2, bf16[768,512]{1,0:T(8,128)(2,1)} %w_hbm.1, s32[1,224]{1,0:T(1,128)} %bitcast.3), custom_call_target="tpu_custom_call" | custom-call | tf_op jit(solution)/shard_map/pallas_call | solution.py:352
  87.6 2.4 %shard_map.60 = (bf16[768,512]{1,0:T(8,128)(2,1)}, bf16[768,512]{1,0:T(8,128)(2,1)}) custom-call(bf16[768,512]{1,0:T(8,128)(2,1)} %get-tuple-element.4.step_ref, bf16[768,512]{1,0:T(8,128)(2,1)} %get-tuple-element.5.resid_ref), custom_call_target="tpu_custom_call" | custom-call | tf_op jit(solution)/shard_map/pallas_call | solution.py:394

commit v8 on v7

--- a/solution.py
+++ b/solution.py
@@ -151,10 +151,11 @@
                 total[j, start:stop] = value[:, j * LANES:(j + 1) * LANES]
 
         times(0, top)
-        extra = ride(1, None)
         to_ya = []
         for j in range(2):
             to_ya.append([send(total.at[j, rows_at(lax.rem(y + k, NY) * pa, pa)], ya.at[j, y], to_y(k)) for k in ORDER_8])
+            if j == 0:
+                extra = ride(1, None)
         times(top, depth)
         to_zb = []
         for k in ORDER_4:

time: 90.2 us -> 89.8 us (level)
  no operation moved by 1% of the time
where the time goes in v8:
time: 89.8 us; the launch traced here: 89.6 us
  Pallas kernels  89 us (99%)
    pallas_call x1, Pallas kernels, body(): pl.pallas_call(kernel, out_shape=(out, out), in_specs=[hbm] * 4, out_spec...  86.5 us
    pallas_call x1, Pallas kernels, body(): pl.pallas_call(write, out_shape=(out, out), in_specs=[hbm] * 2, out_specs...  2.44 us

profile of v8, /device:TPU:1, one launch (start us, length us, event | category | flops | bytes accessed | tf_op | source)
XLA Modules:
  0.0 89.6 jit_solution(9832143216301596636)
XLA Ops:
  0.6 86.5 %shard_map.59 = (bf16[768,512]{1,0:T(8,128)(2,1)}, bf16[768,512]{1,0:T(8,128)(2,1)}) custom-call(bf16[256,768]{1,0:T(8,128)(2,1)} %x_hbm.1, s32[1,256]{1,0:T(1,128)} %bitcast.2, bf16[768,512]{1,0:T(8,128)(2,1)} %w_hbm.1, s32[1,224]{1,0:T(1,128)} %bitcast.3), custom_call_target="tpu_custom_call" | custom-call | tf_op jit(solution)/shard_map/pallas_call | solution.py:353
  87.2 2.4 %shard_map.60 = (bf16[768,512]{1,0:T(8,128)(2,1)}, bf16[768,512]{1,0:T(8,128)(2,1)}) custom-call(bf16[768,512]{1,0:T(8,128)(2,1)} %get-tuple-element.4.step_ref, bf16[768,512]{1,0:T(8,128)(2,1)} %get-tuple-element.5.resid_ref), custom_call_target="tpu_custom_call" | custom-call | tf_op jit(solution)/shard_map/pallas_call | solution.py:395

commit v9 on v8

--- a/solution.py
+++ b/solution.py
@@ -128,10 +128,11 @@
         err_out[lax.rem(core + side, 2)] = ((p - jnp.where(label == class_id, 1.0, 0.0)) / total_rows).astype(BF16)
 
     def to_chips(out, into):
-        copies = [send(out.at[1], into.at[1, feat], partner)]
+        copies = []
         for k in ORDER_8:
             copies.append(send(out.at[0], into.at[0, feat], to_feat(k)))
             copies.append(send(out.at[1], into.at[1, feat], to_other(k)))
+        copies.append(send(out.at[1], into.at[1, feat], partner))
         into[0, feat] = out[0]
         return copies
 

time: 89.8 us -> 90 us (level)
  no operation moved by 1% of the time
where the time goes in v9:
time: 90 us; the launch traced here: 89.8 us
  Pallas kernels  89.2 us (99%)
    pallas_call x1, Pallas kernels, body(): pl.pallas_call(kernel, out_shape=(out, out), in_specs=[hbm] * 4, out_spec...  86.7 us
    pallas_call x1, Pallas kernels, body(): pl.pallas_call(write, out_shape=(out, out), in_specs=[hbm] * 2, out_specs...  2.44 us

profile of v9, /device:TPU:1, one launch (start us, length us, event | category | flops | bytes accessed | tf_op | source)
XLA Modules:
  0.0 89.8 jit_solution(18295670420813396946)
XLA Ops:
  0.6 86.7 %shard_map.59 = (bf16[768,512]{1,0:T(8,128)(2,1)}, bf16[768,512]{1,0:T(8,128)(2,1)}) custom-call(bf16[256,768]{1,0:T(8,128)(2,1)} %x_hbm.1, s32[1,256]{1,0:T(1,128)} %bitcast.2, bf16[768,512]{1,0:T(8,128)(2,1)} %w_hbm.1, s32[1,224]{1,0:T(1,128)} %bitcast.3), custom_call_target="tpu_custom_call" | custom-call | tf_op jit(solution)/shard_map/pallas_call | solution.py:354
  87.4 2.4 %shard_map.60 = (bf16[768,512]{1,0:T(8,128)(2,1)}, bf16[768,512]{1,0:T(8,128)(2,1)}) custom-call(bf16[768,512]{1,0:T(8,128)(2,1)} %get-tuple-element.4.step_ref, bf16[768,512]{1,0:T(8,128)(2,1)} %get-tuple-element.5.resid_ref), custom_call_target="tpu_custom_call" | custom-call | tf_op jit(solution)/shard_map/pallas_call | solution.py:396
